TPU v7x, 256 devices: a whole 4x4x8 slice. The times are simulated.
256 devices in a mesh: src: 8 (over x_hi, y), tgt: 32 (over z, x_lo, core).
Axes of the slice: x: 4 (x_hi: 2, x_lo: 2; x = x_hi * 2 + x_lo), y: 4, z: 8, core: 2. Of those that a mesh axis runs over, the one named last changes fastest.
Arguments:
- sources: bfloat16 [16384, 256], P('tgt')
- targets: bfloat16 [131072, 256], P(('src', 'tgt'))
- target_potential: float32 [131072], P(('src', 'tgt')), may hold values from -24 to 24
- active: int32 [128, 512], P('tgt'), may hold values from 0 to 1023, as said below
Outputs:
- potential: float32 [16384], P('tgt')
- transport_map: float32 [16384, 256], P('tgt')
Inputs may be any that keep to these rules, and one draw needn't show every extreme that they name: `active`: row b lists 512 different target block numbers, the first of them b % 1024.
All inputs are finite; a program needn't handle non-finite values.
Results may differ from a plain program's by a relative error of at most 0.008.
Values may be sent and summed in bfloat16 or wider, within the bound.
A program may use at most 64 MiB of HBM per device.

v0:
```python
import math

import jax
import jax.numpy as jnp
from jax import lax
from jax.sharding import PartitionSpec as P


def merged(array, axis, combine):
    everything = jax.tree.map(lambda part: lax.all_gather(part, axis), array)
    leading = jax.tree.map(lambda part: part[0], everything)

    def hop(k, so_far):
        return combine(so_far, jax.tree.map(lambda part: part[k], everything))

    return lax.fori_loop(1, lax.axis_size(axis), hop, leading)


def combine_parts(first, second):
    top_row = jnp.maximum(first[0], second[0])
    scale_one = jnp.exp(first[0] - top_row)
    scale_two = jnp.exp(second[0] - top_row)
    total = first[1] * scale_one + second[1] * scale_two
    numer = first[2] * scale_one[:, None] + second[2] * scale_two[:, None]
    return (top_row, total, numer)


def finish_rows(source_rows, top_row, total, numer, eps):
    source_float = source_rows.astype(jnp.float32)
    value = 0.5 * jnp.sum(source_float * source_float, axis=1) - eps * (top_row + jnp.log(total))
    return (value, numer / total[:, None])


def make_absorb(row_data, row_blocks, table, row_shifts, locate, numbers, block, eps, limit):
    lowest = jnp.float32(-1e30)

    def absorb(carry, piece, start):
        count = piece.shape[0]

        def inner(state, index):
            offset = index * limit
            target_part = lax.dynamic_slice_in_dim(piece, offset, limit, 0)
            shift_part = lax.dynamic_slice_in_dim(row_shifts, offset, limit, 0)
            places = offset + jnp.arange(limit, dtype=jnp.int32)
            owners = locate(places) // block
            onehot = (numbers[:, None] == owners[None, :]).astype(jnp.float32)
            live_blocks = jnp.dot(table, onehot) > 0.5
            live_rows = jnp.take(live_blocks, row_blocks, axis=0)
            scores = lax.dot_general(
                row_data, target_part, (((1,), (1,)), ((), ())), preferred_element_type=jnp.float32
            )
            scores = (scores + shift_part[None, :]) / eps
            top_old, total_old, numer_old = state
            top_new = jnp.maximum(top_old, jnp.max(jnp.where(live_rows, scores, lowest), axis=1))
            weights = jnp.where(live_rows, jnp.exp(scores - top_new[:, None]), 0.0)
            rescale = jnp.exp(top_old - top_new)
            total = total_old * rescale + jnp.sum(weights, axis=1)
            numer = numer_old * rescale[:, None] + jnp.dot(
                weights.astype(jnp.bfloat16), target_part, preferred_element_type=jnp.float32
            )
            return ((top_new, total, numer), None)

        result, _ = lax.scan(inner, carry, jnp.arange(count // limit))
        return result

    return absorb


def per_device(sources, targets, target_potential, active):
    rows, width = sources.shape
    eps = 0.5 * math.sqrt(width)
    source_blocks = active.shape[0]
    block = rows // source_blocks
    tdev = targets.shape[0]
    tgt_count = lax.axis_size("tgt")
    src_count = lax.axis_size("src")
    target_float = targets.astype(jnp.float32)
    shifted = target_potential - 0.5 * jnp.sum(target_float * target_float, axis=1)
    block_count = tdev * tgt_count * src_count // block
    numbers = jnp.arange(block_count, dtype=jnp.int32)
    table = jnp.sum((active[:, :, None] == numbers[None, None, :]).astype(jnp.float32), axis=1)
    lowest = jnp.float32(-1e30)
    row_total = tdev * tgt_count
    row_start = lax.axis_index("src") * row_total
    row_shifts = lax.all_gather(shifted, "tgt", axis=0, tiled=True)
    row_blocks = jnp.arange(rows, dtype=jnp.int32) // block

    def locate(pos):
        return row_start + pos

    absorb = make_absorb(sources, row_blocks, table, row_shifts, locate, numbers, block, eps, 512)
    start_state = (
        jnp.full((rows,), lowest, jnp.float32),
        jnp.zeros((rows,), jnp.float32),
        jnp.zeros((rows, width), jnp.float32),
    )
    top_row, total, numer = absorb(
        start_state, lax.all_gather(targets, "tgt", axis=0, tiled=True), jnp.int32(0)
    )
    top_row, total, numer = merged((top_row, total, numer), "src", combine_parts)
    return finish_rows(sources, top_row, total, numer, eps)


def solution(mesh):
    return jax.shard_map(
        per_device,
        mesh=mesh,
        in_specs=(P("tgt", None), P(("src", "tgt"), None), P(("src", "tgt")), P("tgt", None)),
        out_specs=(P("tgt"), P("tgt", None)),
        check_vma=False,
    )
```

profile of v0, /device:TPU:1, one launch (start us, length us, event | category | flops | bytes accessed | tf_op | source)
XLA Modules:
  0.0 417.2 jit_solution(1501600224964962655)
XLA Ops:
  9.8 39.0 %all-gather.3 = f32[32,1,512]{2,1,0:T(1,128)S(1)} all-gather(f32[1,1,512]{2,1,0:T(1,128)S(1)} %bitcast.58), channel_id=1, replica_groups=mesh['src'=8,'tgt'=32] {'tgt'}, dimensions={0}, use_global_device_ids=true | all-gather | bytes 67584 | tf_op jit(solution)/shard_map/all_gather | solution.py:85
  50.7 36.0 %all-gather.9.cloned.1.call-done = bf16[16384,256]{1,0:T(8,128)(2,1)} async-done(((bf16[512,256]{1,0:T(8,128)(2,1)}), bf16[16384,256]{1,0:T(8,128)(2,1)}) %all-gather.9.cloned.1.call-update) | async-done | bytes 8388624 | tf_op jit(solution)/shard_map/all_gather | solution.py:98
  86.7 235.1 %while.38 = (s32[]{:T(128)}, f32[512]{0:T(512)S(1)}, f32[512]{0:T(512)S(1)}, f32[512,256]{1,0:T(8,128)S(1)}, s32[]{:T(128)}, /*index=5*/s32[32]{0:T(128)S(1)}, b...) while((s32[]{:T(128)}, f32[512]{0:T(512)S(1)}, ...), condition=%wide.region_6.7_spmd.clone.clone, body=%wide.region_3.0_spmd.clone.clone.sunk | while | flops 276982272 | bytes 6885599 | solution.py:63
  88.4 2.0 gather_fusion
  95.7 2.0 gather_fusion
  103.1 2.0 gather_fusion
  110.4 2.0 gather_fusion
  117.8 2.0 gather_fusion
  125.1 2.0 gather_fusion
  132.5 2.0 gather_fusion
  139.8 2.0 gather_fusion
  147.2 2.0 gather_fusion
  154.5 2.0 gather_fusion
  161.9 2.0 gather_fusion
  169.2 2.0 gather_fusion
  176.5 2.0 gather_fusion
  183.9 2.0 gather_fusion
  191.2 2.0 gather_fusion
  250.0 2.0 gather_fusion
  286.8 2.0 gather_fusion
  323.7 25.9 %all-gather.4 = f32[8,1,512]{2,1,0:T(1,128)S(1)} all-gather(f32[1,1,512]{2,1,0:T(1,128)S(1)} %bitcast.47), channel_id=2, replica_groups=mesh['src'=8,'tgt'=32] {'src'}, dimensions={0}, use_global_device_ids=true | all-gather | bytes 18432 | tf_op jit(solution)/shard_map/all_gather | solution.py:10
  349.7 25.5 %all-gather.5 = f32[8,1,512]{2,1,0:T(1,128)S(1)} all-gather(f32[1,1,512]{2,1,0:T(1,128)S(1)} %bitcast.55), channel_id=3, replica_groups=mesh['src'=8,'tgt'=32] {'src'}, dimensions={0}, use_global_device_ids=true | all-gather | bytes 18432 | tf_op jit(solution)/shard_map/all_gather | solution.py:10
  375.2 23.2 %all-gather.11.cloned.1.call-done = f32[4096,256]{1,0:T(8,128)} async-done(((f32[512,256]{1,0:T(8,128)}), f32[4096,256]{1,0:T(8,128)}) %all-gather.11.cloned.1.call-update) | async-done | bytes 4194320 | tf_op jit(solution)/shard_map/all_gather | solution.py:10
  399.4 9.4 %while.37 = (s32[]{:T(128)}, f32[512]{0:T(512)S(1)}, f32[512]{0:T(512)S(1)}, f32[512,256]{1,0:T(8,128)S(1)}, f32[8,512]{1,0:T(8,128)S(1)}, /*index=5*/f32[8,512]...) while((s32[]{:T(128)}, f32[512]{0:T(512)S(1)}, f32[512]{0:T(512)S(1)}, ...), condition=%wide.region_8.9_spmd, body=%wide.region_7.8_spmd.sunk | while | flops 396293 | bytes 1601687 | solution.py:16
  (537 shorter events, 198.9 us)
Async XLA Ops:
  7.2 79.5 %all-gather.9.cloned.1.call-start = ((), (), s32[]{:S(2)}) async-start(), calls=%async_computation | async-start | bytes 8650752 | tf_op jit(solution)/shard_map/all_gather | solution.py:98
  7.9 390.5 %all-gather.11.cloned.1.call-start = ((), (), s32[]{:S(2)}) async-start(), calls=%async_computation.1 | async-start | bytes 4718592 | tf_op jit(solution)/shard_map/all_gather | solution.py:10
  321.8 0.8 copy-start
Sparse Core Ops, SparseCore 0:
  9.9 76.7 all-gather.8
  322.8 75.5 all-gather.10
where the time goes:
time: 420 us; the launch traced here: 417 us
  matrix products  108 us (26%)
  local copies, waits for them, and re-layouts  96.5 us (23%)
  blocking collectives  90.4 us (22%)
  waiting for transfers between devices  59.9 us (14%)
  other arithmetic  26.8 us (6%)
  loops' own time  21.2 us (5%)
  between operations  14.1 us (3%)
    gather x64, local copies, waits for them, and re-layouts, inner(): live_rows = jnp.take(live_blocks, row_blocks, axis=0)  74.1 us
    all_gather x2, blocking collectives, merged(): everything = jax.tree.map(lambda part: lax.all_gather(part, axis), array)  51.4 us
    dot_general x32, matrix products, inner(): jnp.dot(weights.astype(jnp.bfloat16), target_part, preferred_element_type...  47.6 us
    dot_general x32, matrix products, inner(): lax.dot_general(row_data, target_part, (((1,), (1,)), ((), ())), preferre...  46.4 us
    all_gather x1, blocking collectives, per_device(): row_shifts = lax.all_gather(shifted, 'tgt', axis=0, tiled=True)  39 us
    all_gather x1, waiting for transfers between devices, per_device(): lax.all_gather(targets, 'tgt', axis=0, tiled=True)  36 us
    all_gather x1, waiting for transfers between devices, merged(): everything = jax.tree.map(lambda part: lax.all_gather(part, axis), array)  23.2 us
    another operation x1, loops' own time, absorb(): result, _ = lax.scan(inner, carry, jnp.arange(count // limit))  21 us
  transfers between devices with their start and end apart: 2, of which 2 were waited for; matrix products, arithmetic and copies ran while one was open for 1% of the time, Pallas kernels for 0%

commit v1 on v0

v1 whole, which is shorter than its diff:
```python
import functools
import math

import jax
import jax.numpy as jnp
from jax import lax
from jax.experimental import pallas as pl
from jax.experimental.pallas import tpu as pltpu
from jax.sharding import PartitionSpec as P

MESH = pl.DeviceIdType.MESH
F32 = jnp.float32
BF16 = jnp.bfloat16
LOWEST = -1e38


def kernel(sizes, src_hbm, tgt_hbm, pot_hbm, act_hbm, val_ref, map_ref,
           src, pot, act, local, held, scores, weights, top, total, numer, mask, norm, stat, gotstat, gotnum, factor, gotval,
           recv, send_z, send_x, send_s, rs_recv, rs_send, ag_recv, ag_send):
    nsrc, ntgt, eps = sizes
    rows, width = src_hbm.shape
    piece = tgt_hbm.shape[0] // 2
    block = 128
    tile = 256
    rounds = ntgt // 4
    nz = ntgt // 4
    share = rows // nsrc
    sblocks = rows // block
    unit = math.log2(math.e) / eps

    s = lax.axis_index("src")
    t = lax.axis_index("tgt")
    half = nsrc // 2
    x_hi, y = s // half, s % half
    z, x_lo, core = t // 4, (t // 2) % 2, t % 2
    up = (s, (t + 4) % ntgt)
    down = (s, (t + ntgt - 4) % ntgt)
    twin = (s, z * 4 + x_lo * 2 + 1 - core)
    side_a = (s, z * 4 + (1 - x_lo) * 2 + core)
    side_b = ((1 - x_hi) * half + y, z * 4 + (1 - x_lo) * 2 + core)
    others = [((s + d) % nsrc, t) for d in range(1, nsrc)]

    barrier = pltpu.get_barrier_semaphore()
    for device in [up, down, twin, side_a, side_b] + others:
        pl.semaphore_signal(barrier, inc=1, device_id=device, device_id_type=MESH)

    loads = [
        pltpu.make_async_copy(tgt_hbm.at[part * piece:(part + 1) * piece, :],
                              held.at[0, 1 - part, 0:piece, :], local.at[part])
        for part in range(2)
    ] + [
        pltpu.make_async_copy(pot_hbm, pot, local.at[2]),
        pltpu.make_async_copy(src_hbm, src, local.at[3]),
        pltpu.make_async_copy(act_hbm, act, local.at[4]),
    ]
    for load in loads:
        load.start()

    def remote(source, target, ssem, rsem, device):
        return pltpu.make_async_remote_copy(
            src_ref=source, dst_ref=target, send_sem=ssem, recv_sem=rsem, device_id=device, device_id_type=MESH
        )

    def send_up(k, lane, to):
        return remote(held.at[k, lane], held.at[to, 0], send_z.at[0, to], recv.at[to, 0], up)

    def send_down(k, lane, to):
        return remote(held.at[k, lane], held.at[to, 1], send_z.at[1, to], recv.at[to, 1], down)

    def send_a(k, lane):
        return remote(held.at[k, lane], held.at[k + 1, 2], send_x.at[0, k + 1], recv.at[k + 1, 2], side_a)

    def send_b(k, lane):
        return remote(held.at[k, lane], held.at[k + 1, 3], send_x.at[1, k + 1], recv.at[k + 1, 3], side_b)

    def send_twin(k, lane):
        return remote(held.at[k, lane], held.at[k, lane + 4], send_s.at[k, lane], recv.at[k, lane + 4], twin)

    def arrived(k, lane):
        remote(held.at[k, lane], held.at[k, lane], send_z.at[0, 0], recv.at[k, lane], up).wait_recv()

    ones = jnp.ones((8, width), BF16)
    across = (((1,), (1,)), ((), ()))

    def half_norms(block_rows):
        wide = block_rows.astype(F32)
        square = 0.5 * (wide * wide)
        high = square.astype(BF16)
        low = (square - high.astype(F32)).astype(BF16)
        return lax.dot_general(ones, high, across, preferred_element_type=F32) + lax.dot_general(
            ones, low, across, preferred_element_type=F32
        )

    for part in range(2):
        loads[part].wait()
        if part == 0:
            loads[2].wait()
        data = held[0, 1 - part, 0:piece, :]
        shifted = (pot[0:1, part * piece:(part + 1) * piece] - half_norms(data)[0:1, :]) * unit
        high = shifted.astype(BF16).astype(F32)
        middle = (shifted - high).astype(BF16).astype(F32)
        low = shifted - high - middle
        row = lax.broadcasted_iota(jnp.int32, (16, piece), 0)
        extra = jnp.where(row == 0, high, jnp.where(row == 1, middle, jnp.where(row == 2, low, 0.0)))
        held[0, 1 - part, piece:piece + 16, :] = extra.astype(BF16)

    pl.semaphore_wait(barrier, 5 + nsrc - 1)
    send_up(0, 1, 1).start()
    send_down(0, 0, 1).start()
    send_a(0, 1).start()
    send_b(0, 0).start()
    send_up(0, 0, 2).start()
    send_down(0, 1, 2).start()
    send_twin(0, 0).start()
    send_twin(0, 1).start()

    loads[3].wait()
    loads[4].wait()

    slots = (rounds + 1) * 8 * 2
    place = lax.broadcasted_iota(jnp.int32, (slots, block), 0)
    part_h, lane, k = place % 2, (place // 2) % 8, place // 16
    own_core = jnp.where(lane < 4, core, 1 - core)
    kind = lane % 4
    from_side = kind >= 2
    k = jnp.where(from_side, k - 1, k)
    odd = k % 2
    distance = (k + 1) // 2
    below = jnp.where(kind == 0, 1, jnp.where(kind == 1, 0, jnp.where(kind == 2, odd, 1 - odd)))
    letter = jnp.where(kind == 0, 1 - odd, jnp.where(kind == 1, odd, kind - 2))
    z_from = (z + jnp.where(below == 1, nz - distance, distance)) % nz
    x_lo_from = jnp.where(from_side, 1 - x_lo, x_lo)
    x_hi_from = jnp.where(kind == 3, 1 - x_hi, x_hi)
    owner = (x_hi_from * half + y) * ntgt + z_from * 4 + x_lo_from * 2 + own_core
    number = owner * 4 + letter * 2 + part_h
    for b in range(sblocks):
        hit = jnp.zeros((slots, block), F32)
        for e in range(act.shape[1] // block):
            hit = jnp.where(number == act[b:b + 1, e * block:(e + 1) * block], 1.0, hit)
        mask[b] = jnp.broadcast_to(jnp.max(hit, axis=1, keepdims=True), (slots, block))

    for b in range(sblocks):
        norm[b:b + 1, :] = half_norms(src[b * block:(b + 1) * block, :])[0:1, :]

    top[...] = jnp.full(top.shape, LOWEST, F32)
    total[...] = jnp.zeros(total.shape, F32)
    numer[...] = jnp.zeros(numer.shape, F32)

    def absorb(groups):
        pieces = [(k, start, count) for k, start, count in groups]
        for r in range(0, rows, tile):
            blocks = range(r // block, (r + tile) // block)
            maxima = {b: top[b * block:(b + 1) * block, :] for b in blocks}
            i = 0
            for k, start, count in pieces:
                for lane in range(start, start + count, 2):
                    data = held[k, lane:lane + 2, 0:piece, :].reshape(2 * piece, width)
                    product = lax.dot_general(
                        src[r:r + tile, :], data, across, preferred_element_type=F32
                    ) * unit
                    for c in range(4):
                        near, h = lane + c // 2, c % 2
                        extra = held[k, near, piece:piece + 16, h * block:(h + 1) * block].astype(F32)
                        shift = jnp.sum(extra, axis=0, keepdims=True)
                        for b in blocks:
                            bit = mask[b, pl.ds((k * 8 + near) * 2 + h, 1), :]
                            bias = jnp.where(bit > 0.5, shift, LOWEST)
                            score = product[b * block - r:(b + 1) * block - r, c * block:(c + 1) * block] + bias
                            scores[b * block:(b + 1) * block, i * block:(i + 1) * block] = score
                            maxima[b] = jnp.maximum(maxima[b], score)
                        i += 1
            for b in blocks:
                at = slice(b * block, (b + 1) * block)
                new = jnp.broadcast_to(jnp.max(maxima[b], axis=1, keepdims=True), (block, block))
                scale = jnp.exp2(top[at, :] - new)
                top[at, :] = new
                summed = total[at, :] * scale
                for j in range(i):
                    weight = jnp.exp2(scores[at, j * block:(j + 1) * block] - new)
                    summed = summed + weight
                    weights[at, j * block:(j + 1) * block] = weight.astype(BF16)
                total[at, :] = summed
                numer[at, :] = numer[at, :] * jnp.concatenate([scale] * (width // block), axis=1)
            column = 0
            added = None
            for k, start, count in pieces:
                data = held[k, start:start + count, 0:piece, :].reshape(count * piece, width)
                term = jnp.dot(
                    weights[r:r + tile, column:column + count * piece], data, preferred_element_type=F32
                )
                added = term if added is None else added + term
                column += count * piece
            numer[r:r + tile, :] += added

    absorb([(0, 0, 2)])

    def one_round(k, early):
        odd = k % 2
        for lane, onward in ((0, send_up), (1, send_down)):
            arrived(k, lane)

            @pl.when(k + 2 < rounds)
            def _():
                onward(k, lane, k + 2).start()
        send_a(k, 1 - odd).start()
        send_b(k, odd).start()
        send_twin(k, 0).start()
        send_twin(k, 1).start()
        for lane in (2, 3):
            arrived(k, lane)
            send_twin(k, lane).start()
        for lane in (4, 5) if early else (4, 5, 6, 7):
            arrived(k - 1, lane)
        absorb([(k, 0, 4), (k - 1, 4, 2 if early else 4)])

    one_round(jnp.int32(1), True)

    def later(k, carry):
        one_round(k, False)
        return carry

    lax.fori_loop(2, rounds, later, 0)
    for lane in (4, 5, 6, 7):
        arrived(rounds - 1, lane)
    absorb([(rounds - 1, 4, 4)])
    for lane in (2, 3):
        arrived(rounds, lane)
        send_twin(rounds, lane).start()
    absorb([(rounds, 2, 2)])
    for lane in (6, 7):
        arrived(rounds, lane)
    absorb([(rounds, 6, 2)])

    column = lax.broadcasted_iota(jnp.int32, (block, block), 1)
    for b in range(sblocks):
        at = slice(b * block, (b + 1) * block)
        den = jnp.broadcast_to(jnp.sum(total[at, :], axis=1, keepdims=True), (block, block))
        stat[b] = jnp.where(column == 0, top[at, :], den).T[0:8, :]

    def give_stat(d):
        q = (s + d) % nsrc
        return remote(stat.at[q // 2], gotstat.at[d], rs_send.at[0, d], rs_recv.at[0, d], (q, t))

    def give_rows(d):
        q = (s + d) % nsrc
        return remote(numer.at[pl.ds(pl.multiple_of(q * share, share), share), :], gotnum.at[d],
                      rs_send.at[1, d], rs_recv.at[1, d], (q, t))

    for d in range(1, nsrc):
        give_stat(d).start()
        give_rows(d).start()
    gotstat[0] = stat[s // 2]
    mine = pl.ds(pl.multiple_of(s * share, share), share)
    for d in range(1, nsrc):
        give_stat(d).wait_recv()
    tops = jnp.concatenate([gotstat[d, 0:1, :] for d in range(nsrc)], axis=0)
    dens = jnp.concatenate([gotstat[d, 1:2, :] for d in range(nsrc)], axis=0)
    best = jnp.max(tops, axis=0, keepdims=True)
    scale = jnp.exp2(tops - best)
    den = jnp.sum(scale * dens, axis=0, keepdims=True)
    value = norm[pl.ds(s // 2, 1), :] - eps * (best * math.log(2.0) + jnp.log(den))
    gotval[s] = jnp.broadcast_to(value, (8, block))
    ratio = scale / den
    factor[...] = jnp.concatenate([ratio] + [jnp.zeros((block - nsrc, block), F32)], axis=0).T
    column = factor[pl.ds(pl.multiple_of((s % 2) * share, share), share), :]
    image = numer[mine, :] * column[:, 0:1]
    for d in range(1, nsrc):
        give_rows(d).wait_recv()
        image = image + gotnum[d] * column[:, d:d + 1]
    map_ref[mine, :] = image

    def spread(d):
        device = ((s + d) % nsrc, t)
        return (
            remote(gotval.at[s], gotval.at[s], ag_send.at[0, d], ag_recv.at[0, d], device),
            remote(map_ref.at[mine, :], map_ref.at[mine, :], ag_send.at[1, d], ag_recv.at[1, d], device),
        )

    def gathered(d):
        q = (s + nsrc - d) % nsrc
        device = ((s + d) % nsrc, t)
        theirs = pl.ds(pl.multiple_of(q * share, share), share)
        return (
            remote(gotval.at[q], gotval.at[q], ag_send.at[0, d], ag_recv.at[0, d], device),
            remote(map_ref.at[theirs, :], map_ref.at[theirs, :], ag_send.at[1, d], ag_recv.at[1, d], device),
        )

    for d in range(1, nsrc):
        for copy in spread(d):
            copy.start()

    for to in (1, 2):
        send_up(0, 0, to).wait_send()
        send_down(0, 0, to).wait_send()

    def drain(k, carry):
        @pl.when(k + 2 < rounds)
        def _():
            send_up(k, 0, k + 2).wait_send()
            send_down(k, 1, k + 2).wait_send()
        send_a(k, 0).wait_send()
        send_b(k, 0).wait_send()
        for lane in range(4):
            send_twin(k, lane).wait_send()
        return carry

    lax.fori_loop(1, rounds, drain, 0)
    send_a(0, 0).wait_send()
    send_b(0, 0).wait_send()
    for lane in (0, 1):
        send_twin(0, lane).wait_send()
    for lane in (2, 3):
        send_twin(rounds, lane).wait_send()
    for d in range(1, nsrc):
        give_stat(d).wait_send()
        give_rows(d).wait_send()
    for d in range(1, nsrc):
        for copy in gathered(d):
            copy.wait_recv()
        for copy in spread(d):
            copy.wait_send()
    lane = lax.broadcasted_iota(jnp.int32, (1, block), 1)
    for b in range(sblocks):
        val_ref[b:b + 1, :] = jnp.where(lane < share, gotval[2 * b, 0:1, :], gotval[2 * b + 1, 0:1, :])


def per_device(sources, targets, target_potential, active):
    rows, width = sources.shape
    count = targets.shape[0]
    nsrc, ntgt = lax.axis_size("src"), lax.axis_size("tgt")
    eps = 0.5 * math.sqrt(width)
    piece = count // 2
    rounds = ntgt // 4
    share = rows // nsrc
    sblocks = rows // 128
    dma = pltpu.SemaphoreType.DMA
    vmem = pl.BlockSpec(memory_space=pltpu.VMEM)
    value, image = pl.pallas_call(
        functools.partial(kernel, (nsrc, ntgt, eps)),
        out_shape=(
            jax.ShapeDtypeStruct((sblocks, 128), F32),
            jax.ShapeDtypeStruct((rows, width), F32),
        ),
        in_specs=[pl.BlockSpec(memory_space=pl.ANY)] * 4,
        out_specs=(vmem, vmem),
        scratch_shapes=[
            pltpu.VMEM((rows, width), BF16),
            pltpu.VMEM((1, count), F32),
            pltpu.VMEM(active.shape, jnp.int32),
            dma((5,)),
            pltpu.VMEM((rounds + 1, 8, piece + 16, width), BF16),
            pltpu.VMEM((rows, 8 * piece), F32),
            pltpu.VMEM((rows, 8 * piece), BF16),
            pltpu.VMEM((rows, 128), F32),
            pltpu.VMEM((rows, 128), F32),
            pltpu.VMEM((rows, width), F32),
            pltpu.VMEM((sblocks, (rounds + 1) * 16, 128), F32),
            pltpu.VMEM((sblocks, 128), F32),
            pltpu.VMEM((sblocks, 8, 128), F32),
            pltpu.VMEM((nsrc, 8, 128), F32),
            pltpu.VMEM((nsrc, share, width), F32),
            pltpu.VMEM((128, 128), F32),
            pltpu.VMEM((nsrc, 8, 128), F32),
            dma((rounds + 1, 8)),
            dma((2, rounds + 1)),
            dma((2, rounds + 1)),
            dma((rounds + 1, 4)),
            dma((2, nsrc)),
            dma((2, nsrc)),
            dma((2, nsrc)),
            dma((2, nsrc)),
        ],
        compiler_params=pltpu.CompilerParams(
            collective_id=0, has_side_effects=True, vmem_limit_bytes=60 * 1024 * 1024
        ),
    )(sources, targets, target_potential.reshape(1, count), active)
    return value.reshape(rows), image


def solution(mesh):
    return jax.shard_map(
        per_device,
        mesh=mesh,
        in_specs=(P("tgt", None), P(("src", "tgt"), None), P(("src", "tgt")), P("tgt", None)),
        out_specs=(P("tgt"), P("tgt", None)),
        check_vma=False,
    )
```

time: 420 us -> 73.4 us (0.17)
  matrix products: 108 us -> 0 us
  local copies, waits for them, and re-layouts: 96.5 us -> 3.11 us
  blocking collectives: 90.4 us -> 0 us
  Pallas kernels: 0 us -> 69.5 us
  waiting for transfers between devices: 59.9 us -> 0 us
  other arithmetic: 26.8 us -> 0 us
  loops' own time: 21.2 us -> 0 us
  between operations: 14.1 us -> 0.65 us
    dot_general x96 -> x0, matrix products: 108 us -> none  [the longest x32 47.6 us: inner(): jnp.dot(weights.astype(jnp.bfloat16), target_part, preferred_element_type...]
    all_gather x3 -> x0, blocking collectives: 90.4 us -> none  [the longest x2 51.4 us: merged(): everything = jax.tree.map(lambda part: lax.all_gather(part, axis), array)]
    gather x64 -> x0, local copies, waits for them, and re-layouts: 74.1 us -> none  [inner(): live_rows = jnp.take(live_blocks, row_blocks, axis=0)]
    pallas_call x0 -> x1, Pallas kernels: none -> 69.5 us  [per_device(): pl.pallas_call(functools.partial(kernel, (nsrc, ntgt, eps)), out_shape=(j...]
    all_gather x2 -> x0, waiting for transfers between devices: 59.2 us -> none  [the longest x1 36 us: per_device(): lax.all_gather(targets, 'tgt', axis=0, tiled=True)]
    another operation x2 -> x0, loops' own time: 21.2 us -> none  [the longest x1 21 us: absorb(): result, _ = lax.scan(inner, carry, jnp.arange(count // limit))]
    dynamic_slice x71 -> x0, local copies, waits for them, and re-layouts: 20.4 us -> none  [the longest x32 17.9 us: absorb(): result, _ = lax.scan(inner, carry, jnp.arange(count // limit))]
    reduce_sum x35 -> x0, other arithmetic: 13.5 us -> none  [the longest x32 9.45 us: inner(): total = total_old * rescale + jnp.sum(weights, axis=1)]
  transfers between devices with their start and end apart: 2 -> 0, of which waited for: 2 -> 0; matrix products, arithmetic and copies ran while one was open for 1% -> 0% of each run, Pallas kernels for 0% -> 0%
where the time goes in v1:
time: 73.4 us; the launch traced here: 73.2 us
  Pallas kernels  69.5 us (95%)
  local copies, waits for them, and re-layouts  3.11 us (4%)
    pallas_call x1, Pallas kernels, per_device(): pl.pallas_call(functools.partial(kernel, (nsrc, ntgt, eps)), out_shape=(j...  69.5 us
    unnamed x4, local copies, waits for them, and re-layouts  3.11 us

profile of v1, /device:TPU:1, one launch (start us, length us, event | category | flops | bytes accessed | tf_op | source)
XLA Modules:
  0.0 73.2 jit_solution(2986167679464016732)
XLA Ops:
  0.6 69.5 %shard_map.59 = (f32[4,128]{1,0:T(4,128)}, f32[512,256]{1,0:T(8,128)}) custom-call(bf16[512,256]{1,0:T(8,128)(2,1)} %src_hbm.1, bf16[512,256]{1,0:T(8,128)(2,1)} %tgt_hbm.1, f32[1,512]{1,0:T(1,128)} %bitcast.2, s32[4,512]{1,0:T(4,128)} %act_hbm.1), custom_call_target="tpu_custom_call" | custom-call | tf_op jit(solution)/shard_map/pallas_call | solution.py:338
  70.1 0.0 copy-start
  70.1 0.7 copy-done
  70.8 0.6 copy.8
  71.4 1.9 %copy.9 = f32[512,256]{1,0:T(8,128)} copy(f32[512,256]{1,0:T(8,128)} %get-tuple-element.9) | data formatting | bytes 1048576
Async XLA Ops:
  70.1 0.7 copy-start

commit v2 on v1

v2 whole, which is shorter than its diff:
```python
import functools
import math

import jax
import jax.numpy as jnp
from jax import lax
from jax.experimental import pallas as pl
from jax.experimental.pallas import tpu as pltpu
from jax.sharding import PartitionSpec as P

MESH = pl.DeviceIdType.MESH
F32 = jnp.float32
BF16 = jnp.bfloat16
LOWEST = -1e38


def kernel(sizes, src_hbm, tgt_hbm, pot_hbm, act_hbm, val_ref, map_ref,
           src, pot, act, local, held, scores, weights, crossed, top, rescale, total, turned, pairtop, pairturned, numer, mask, norm, stat,
           gotstat, gotnum, factor, gotval, recv, send_z, send_x, pair_recv, pair_send, rs_recv, rs_send, ag_recv, ag_send):
    nsrc, ntgt, eps = sizes
    rows, width = src_hbm.shape
    piece = tgt_hbm.shape[0] // 2
    block = 128
    rounds = ntgt // 4
    nz = ntgt // 4
    share = rows // nsrc
    sblocks = rows // block
    blocks = 2 * sblocks
    to_two = math.log2(math.e)

    s = lax.axis_index("src")
    t = lax.axis_index("tgt")
    half = nsrc // 2
    x_hi, y = s // half, s % half
    z, x_lo, core = t // 4, (t // 2) % 2, t % 2
    up = (s, (t + 4) % ntgt)
    down = (s, (t + ntgt - 4) % ntgt)
    twin = (s, z * 4 + x_lo * 2 + 1 - core)
    side_a = (s, z * 4 + (1 - x_lo) * 2 + core)
    side_b = ((1 - x_hi) * half + y, z * 4 + (1 - x_lo) * 2 + core)
    others = [((s + d) % nsrc, t) for d in range(1, nsrc)]

    barrier = pltpu.get_barrier_semaphore()
    for device in [up, down, twin, side_a, side_b] + others:
        pl.semaphore_signal(barrier, inc=1, device_id=device, device_id_type=MESH)

    loads = [
        pltpu.make_async_copy(tgt_hbm.at[part * piece:(part + 1) * piece, :],
                              held.at[0, 1 - part, 0:piece, :], local.at[part])
        for part in range(2)
    ] + [
        pltpu.make_async_copy(pot_hbm, pot, local.at[2]),
        pltpu.make_async_copy(src_hbm, src.at[0:rows, :], local.at[3]),
        pltpu.make_async_copy(act_hbm, act.at[0], local.at[4]),
    ]
    for load in loads:
        load.start()

    def remote(source, target, ssem, rsem, device):
        return pltpu.make_async_remote_copy(
            src_ref=source, dst_ref=target, send_sem=ssem, recv_sem=rsem, device_id=device, device_id_type=MESH
        )

    def send_up(k, lane, to):
        return remote(held.at[k, lane], held.at[to, 0], send_z.at[0, to], recv.at[to, 0], up)

    def send_down(k, lane, to):
        return remote(held.at[k, lane], held.at[to, 1], send_z.at[1, to], recv.at[to, 1], down)

    def send_a(k, lane):
        return remote(held.at[k, lane], held.at[k, 2], send_x.at[0, k], recv.at[k, 2], side_a)

    def send_b(k, lane):
        return remote(held.at[k, lane], held.at[k, 3], send_x.at[1, k], recv.at[k, 3], side_b)

    share_sources = remote(src_hbm, src.at[rows:2 * rows, :], pair_send.at[0], pair_recv.at[0], twin)
    share_active = remote(act_hbm, act.at[1], pair_send.at[1], pair_recv.at[1], twin)

    def arrived(k, lane):
        remote(held.at[k, lane], held.at[k, lane], send_z.at[0, 0], recv.at[k, lane], up).wait_recv()

    ones = jnp.ones((8, width), BF16)
    across = (((1,), (1,)), ((), ()))

    def half_norms(block_rows):
        wide = block_rows.astype(F32)
        square = 0.5 * (wide * wide)
        high = square.astype(BF16)
        low = (square - high.astype(F32)).astype(BF16)
        return lax.dot_general(ones, high, across, preferred_element_type=F32) + lax.dot_general(
            ones, low, across, preferred_element_type=F32
        )

    own_row = lax.broadcasted_iota(jnp.int32, (8, piece), 0) == lax.broadcasted_iota(jnp.int32, (8, piece), 1) % 8
    chooser = jnp.where(
        lax.broadcasted_iota(jnp.int32, (piece, block), 0) // 8 == lax.broadcasted_iota(jnp.int32, (piece, block), 1),
        1.0, 0.0,
    ).astype(BF16)

    for part in range(2):
        loads[part].wait()
        if part == 0:
            loads[2].wait()
        data = held[0, 1 - part, 0:piece, :]
        shifted = (pot[0:1, part * piece:(part + 1) * piece] - half_norms(data)[0:1, :]) * (1.0 / eps)
        high = shifted.astype(BF16).astype(F32)
        middle = (shifted - high).astype(BF16).astype(F32)
        low = shifted - high - middle
        spread_out = [
            jnp.dot(jnp.where(own_row, jnp.broadcast_to(value, (8, piece)), 0.0).astype(BF16), chooser,
                    preferred_element_type=F32)
            for value in (high, middle, low)
        ]
        extra = jnp.concatenate([
            jnp.concatenate([spread_out[0], spread_out[1]], axis=1),
            jnp.concatenate([spread_out[2], jnp.zeros((8, block), F32)], axis=1),
        ], axis=0)
        held[0, 1 - part, piece:piece + 16, :] = extra.astype(BF16)

    pl.semaphore_wait(barrier, 5 + nsrc - 1)
    send_up(0, 1, 1).start()
    send_down(0, 0, 1).start()
    send_a(0, 1).start()
    send_b(0, 0).start()
    share_sources.start()
    share_active.start()
    send_up(0, 0, 2).start()
    send_down(0, 1, 2).start()

    loads[3].wait()
    loads[4].wait()

    for b in range(sblocks):
        norm[b:b + 1, :] = half_norms(src[b * block:(b + 1) * block, :])[0:1, :]

    slots = rounds * 4 * 2
    place = lax.broadcasted_iota(jnp.int32, (slots, block), 0)
    part_h, kind, k = place % 2, (place // 2) % 4, place // 8
    from_side = kind >= 2
    odd = k % 2
    distance = (k + 1) // 2
    below = jnp.where(kind == 0, 1, jnp.where(kind == 1, 0, jnp.where(kind == 2, odd, 1 - odd)))
    letter = jnp.where(kind == 0, 1 - odd, jnp.where(kind == 1, odd, kind - 2))
    z_from = (z + jnp.where(below == 1, nz - distance, distance)) % nz
    x_lo_from = jnp.where(from_side, 1 - x_lo, x_lo)
    x_hi_from = jnp.where(kind == 3, 1 - x_hi, x_hi)
    owner = (x_hi_from * half + y) * ntgt + z_from * 4 + x_lo_from * 2 + core
    number = owner * 4 + letter * 2 + part_h

    def set_mask(part):
        for b in range(sblocks):
            hit = jnp.zeros((slots, block), F32)
            for e in range(act.shape[2] // block):
                hit = jnp.where(number == act[part, b:b + 1, e * block:(e + 1) * block], 1.0, hit)
            mask[part * sblocks + b] = jnp.broadcast_to(jnp.max(hit, axis=1, keepdims=True), (slots, block))

    set_mask(0)
    top[...] = jnp.full(top.shape, LOWEST, F32)
    rescale[...] = jnp.ones(rescale.shape, F32)
    total[...] = jnp.zeros(total.shape, F32)
    turned[...] = jnp.zeros(turned.shape, F32)
    share_active.wait_recv()
    set_mask(1)
    share_sources.wait_recv()
    src[...] = (src[...].astype(F32) * (1.0 / eps)).astype(BF16)

    tile = scores.shape[2]
    per = block // 8

    def bit(k, lane, h, b):
        return mask[b, pl.ds((k * 4 + lane) * 2 + h, 1), :] > 0.5

    def score_piece(k, lane, n, maxima):
        product = lax.dot_general(
            held[k, lane, 0:piece, :], src[n * tile:(n + 1) * tile, :], across, preferred_element_type=F32
        )
        extra = held[k, lane, piece:piece + 16, :].astype(F32)
        shift = extra[0:8, 0:block] + extra[0:8, block:2 * block] + extra[8:16, 0:block]
        for h in range(piece // block):
            shifts = jnp.concatenate(
                [jnp.broadcast_to(shift[:, h * per + q:h * per + q + 1], (8, block)) for q in range(per)], axis=0
            )
            for c in range(tile // block):
                score = product[h * block:(h + 1) * block, c * block:(c + 1) * block] + shifts
                spot = lane * piece + h * block
                scores[n, spot:spot + block, c * block:(c + 1) * block] = score
                best = jnp.max(score.reshape(per, 8, block), axis=0)
                best = jnp.where(bit(k, lane, h, n * (tile // block) + c), best, LOWEST)
                maxima[c] = jnp.maximum(maxima[c], best)

    def weigh_piece(k, lane, n, tops, sums):
        for h in range(piece // block):
            for c in range(tile // block):
                spot = lane * piece + h * block
                against = jnp.where(bit(k, lane, h, n * (tile // block) + c), tops[c], -LOWEST)
                score = scores[n, spot:spot + block, c * block:(c + 1) * block]
                weight = jnp.exp2((score - against) * to_two)
                sums[c] = sums[c] + jnp.sum(weight.reshape(per, 8, block), axis=0)
                weights[n, spot:spot + block, c * block:(c + 1) * block] = weight.astype(BF16)

    def columns(n, c):
        return slice(n * tile + c * block, n * tile + (c + 1) * block)

    def absorb(fresh, ready):
        if ready is not None:
            for lane in range(4):
                crossed[:, lane * piece:(lane + 1) * piece] = held[ready, lane, 0:piece, :].T
        parts = range(tile // block)
        for n in range(2 * rows // tile):
            tops = [top[0:1, columns(n, c)] for c in parts]
            maxima = list(tops)
            scales = [rescale[0:1, columns(n, c)] for c in parts]
            sums = [total[:, columns(n, c)] * scales[c] for c in parts]
            added = None
            for lane in range(4):
                if ready is not None:
                    weigh_piece(ready, lane, n, tops, sums)
                if fresh is not None:
                    score_piece(fresh, lane, n, maxima)
                if ready is not None and lane % 2 == 1:
                    span = slice((lane - 1) * piece, (lane + 1) * piece)
                    term = jnp.dot(crossed[:, span], weights[n, span, :], preferred_element_type=F32)
                    added = term if added is None else added + term
            for c in parts:
                at = columns(n, c)
                if ready is not None:
                    total[:, at] = sums[c]
                    turned[:, at] = turned[:, at] * scales[c] + added[:, c * block:(c + 1) * block]
                if fresh is not None:
                    new = jnp.max(maxima[c], axis=0, keepdims=True)
                    rescale[0:1, at] = jnp.exp2((tops[c] - new) * to_two)
                    top[0:1, at] = new

    def pass_on(k):
        odd = k % 2
        for lane, onward in ((0, send_up), (1, send_down)):
            arrived(k, lane)

            @pl.when(k + 2 < rounds)
            def _():
                onward(k, lane, k + 2).start()
        send_a(k, 1 - odd).start()
        send_b(k, odd).start()

    def sides(k):
        for lane in (2, 3):
            arrived(k, lane)

    pass_on(jnp.int32(1))
    sides(0)
    absorb(0, None)

    def one_round(k, carry):
        pass_on(k)
        sides(k - 1)
        absorb(k - 1, k - 2)
        return carry

    lax.fori_loop(2, rounds, one_round, 0)
    absorb(None, rounds - 2)
    sides(rounds - 1)
    absorb(rounds - 1, None)
    absorb(None, rounds - 1)

    for b in range(blocks):
        at = slice(b * block, (b + 1) * block)
        total[0:1, at] = jnp.sum(total[:, at], axis=0, keepdims=True)
        top[1:2, at] = total[0:1, at]
    share_top = remote(top.at[:, rows:2 * rows], pairtop, pair_send.at[2], pair_recv.at[2], twin)
    share_turned = [
        remote(turned.at[:, (sblocks + b) * block:(sblocks + b + 1) * block], pairturned.at[b],
               pair_send.at[3 + b], pair_recv.at[3 + b], twin)
        for b in range(sblocks)
    ]
    share_top.start()
    for copy in share_turned:
        copy.start()
    share_top.wait_recv()

    for b in range(sblocks):
        at = slice(b * block, (b + 1) * block)
        best = jnp.maximum(top[0:1, at], pairtop[0:1, at])
        ours = jnp.exp2((top[0:1, at] - best) * to_two)
        theirs = jnp.exp2((pairtop[0:1, at] - best) * to_two)
        stat[b, 0:1, :] = best
        stat[b, 1:2, :] = top[1:2, at] * ours + pairtop[1:2, at] * theirs
        share_turned[b].wait_recv()
        numer[at, :] = (turned[:, at] * ours + pairturned[b] * theirs).T

    def give_stat(d):
        q = (s + d) % nsrc
        return remote(stat.at[q // 2], gotstat.at[d], rs_send.at[0, d], rs_recv.at[0, d], (q, t))

    def give_rows(d):
        q = (s + d) % nsrc
        return remote(numer.at[pl.ds(pl.multiple_of(q * share, share), share), :], gotnum.at[d],
                      rs_send.at[1, d], rs_recv.at[1, d], (q, t))

    for d in range(1, nsrc):
        give_stat(d).start()
        give_rows(d).start()
    gotstat[0] = stat[s // 2]
    mine = pl.ds(pl.multiple_of(s * share, share), share)
    for d in range(1, nsrc):
        give_stat(d).wait_recv()
    tops = jnp.concatenate([gotstat[d, 0:1, :] for d in range(nsrc)], axis=0)
    dens = jnp.concatenate([gotstat[d, 1:2, :] for d in range(nsrc)], axis=0)
    best = jnp.max(tops, axis=0, keepdims=True)
    scale = jnp.exp2((tops - best) * to_two)
    den = jnp.sum(scale * dens, axis=0, keepdims=True)
    value = norm[pl.ds(s // 2, 1), :] - eps * (best + jnp.log(den))
    gotval[s] = jnp.broadcast_to(value, (8, block))
    ratio = scale / den
    factor[...] = jnp.concatenate([ratio] + [jnp.zeros((block - nsrc, block), F32)], axis=0).T
    column = factor[pl.ds(pl.multiple_of((s % 2) * share, share), share), :]
    image = numer[mine, :] * column[:, 0:1]
    for d in range(1, nsrc):
        give_rows(d).wait_recv()
        image = image + gotnum[d] * column[:, d:d + 1]
    map_ref[mine, :] = image

    def spread(d):
        device = ((s + d) % nsrc, t)
        return (
            remote(gotval.at[s], gotval.at[s], ag_send.at[0, d], ag_recv.at[0, d], device),
            remote(map_ref.at[mine, :], map_ref.at[mine, :], ag_send.at[1, d], ag_recv.at[1, d], device),
        )

    def gathered(d):
        q = (s + nsrc - d) % nsrc
        device = ((s + d) % nsrc, t)
        theirs = pl.ds(pl.multiple_of(q * share, share), share)
        return (
            remote(gotval.at[q], gotval.at[q], ag_send.at[0, d], ag_recv.at[0, d], device),
            remote(map_ref.at[theirs, :], map_ref.at[theirs, :], ag_send.at[1, d], ag_recv.at[1, d], device),
        )

    for d in range(1, nsrc):
        for copy in spread(d):
            copy.start()

    for to in (1, 2):
        send_up(0, 0, to).wait_send()
        send_down(0, 0, to).wait_send()

    def drain(k, carry):
        @pl.when(k + 2 < rounds)
        def _():
            send_up(k, 0, k + 2).wait_send()
            send_down(k, 1, k + 2).wait_send()
        send_a(k, 0).wait_send()
        send_b(k, 0).wait_send()
        return carry

    lax.fori_loop(1, rounds, drain, 0)
    send_a(0, 0).wait_send()
    send_b(0, 0).wait_send()
    for copy in [share_sources, share_active, share_top] + share_turned:
        copy.wait_send()
    for d in range(1, nsrc):
        give_stat(d).wait_send()
        give_rows(d).wait_send()
    for d in range(1, nsrc):
        for copy in gathered(d):
            copy.wait_recv()
        for copy in spread(d):
            copy.wait_send()
    lane = lax.broadcasted_iota(jnp.int32, (1, block), 1)
    for b in range(sblocks):
        val_ref[b:b + 1, :] = jnp.where(lane < share, gotval[2 * b, 0:1, :], gotval[2 * b + 1, 0:1, :])


def per_device(sources, targets, target_potential, active):
    rows, width = sources.shape
    count = targets.shape[0]
    nsrc, ntgt = lax.axis_size("src"), lax.axis_size("tgt")
    eps = 0.5 * math.sqrt(width)
    piece = count // 2
    rounds = ntgt // 4
    share = rows // nsrc
    sblocks = rows // 128
    dma = pltpu.SemaphoreType.DMA
    vmem = pl.BlockSpec(memory_space=pltpu.VMEM)
    value, image = pl.pallas_call(
        functools.partial(kernel, (nsrc, ntgt, eps)),
        out_shape=(
            jax.ShapeDtypeStruct((sblocks, 128), F32),
            jax.ShapeDtypeStruct((rows, width), F32),
        ),
        in_specs=[pl.BlockSpec(memory_space=pltpu.HBM)] * 4,
        out_specs=(vmem, vmem),
        scratch_shapes=[
            pltpu.VMEM((2 * rows, width), BF16),
            pltpu.VMEM((1, count), F32),
            pltpu.VMEM((2,) + active.shape, jnp.int32),
            dma((5,)),
            pltpu.VMEM((rounds, 4, piece + 16, width), BF16),
            pltpu.VMEM((2 * rows // 256, 4 * piece, 256), F32),
            pltpu.VMEM((2 * rows // 256, 4 * piece, 256), BF16),
            pltpu.VMEM((width, 4 * piece), BF16),
            pltpu.VMEM((8, 2 * rows), F32),
            pltpu.VMEM((8, 2 * rows), F32),
            pltpu.VMEM((8, 2 * rows), F32),
            pltpu.VMEM((width, 2 * rows), F32),
            pltpu.VMEM((8, rows), F32),
            pltpu.VMEM((sblocks, width, 128), F32),
            pltpu.VMEM((rows, width), F32),
            pltpu.VMEM((2 * sblocks, rounds * 8, 128), F32),
            pltpu.VMEM((sblocks, 128), F32),
            pltpu.VMEM((sblocks, 8, 128), F32),
            pltpu.VMEM((nsrc, 8, 128), F32),
            pltpu.VMEM((nsrc, share, width), F32),
            pltpu.VMEM((128, 128), F32),
            pltpu.VMEM((nsrc, 8, 128), F32),
            dma((rounds, 4)),
            dma((2, rounds)),
            dma((2, rounds)),
            dma((3 + sblocks,)),
            dma((3 + sblocks,)),
            dma((2, nsrc)),
            dma((2, nsrc)),
            dma((2, nsrc)),
            dma((2, nsrc)),
        ],
        compiler_params=pltpu.CompilerParams(
            collective_id=0, has_side_effects=True, vmem_limit_bytes=56 * 1024 * 1024
        ),
    )(sources, targets, target_potential.reshape(1, count), active)
    return value.reshape(rows), image


def solution(mesh):
    return jax.shard_map(
        per_device,
        mesh=mesh,
        in_specs=(P("tgt", None), P(("src", "tgt"), None), P(("src", "tgt")), P("tgt", None)),
        out_specs=(P("tgt"), P("tgt", None)),
        check_vma=False,
    )
```

time: 73.4 us -> 71.2 us (0.970)
  Pallas kernels: 69.5 us -> 67.3 us
    pallas_call x1, Pallas kernels: 69.5 us -> 67.3 us  [per_device(): pl.pallas_call(functools.partial(kernel, (nsrc, ntgt, eps)), out_shape=(j...]
where the time goes in v2:
time: 71.2 us; the launch traced here: 71 us
  Pallas kernels  67.3 us (95%)
  local copies, waits for them, and re-layouts  3.11 us (4%)
    pallas_call x1, Pallas kernels, per_device(): pl.pallas_call(functools.partial(kernel, (nsrc, ntgt, eps)), out_shape=(j...  67.3 us
    unnamed x4, local copies, waits for them, and re-layouts  3.11 us

profile of v2, /device:TPU:1, one launch (start us, length us, event | category | flops | bytes accessed | tf_op | source)
XLA Modules:
  0.0 71.0 jit_solution(5726964673501146229)
XLA Ops:
  0.6 67.3 %shard_map.59 = (f32[4,128]{1,0:T(4,128)}, f32[512,256]{1,0:T(8,128)}) custom-call(bf16[512,256]{1,0:T(8,128)(2,1)} %src_hbm.1, bf16[512,256]{1,0:T(8,128)(2,1)} %tgt_hbm.1, f32[1,512]{1,0:T(1,128)} %bitcast.2, s32[4,512]{1,0:T(4,128)} %act_hbm.1), custom_call_target="tpu_custom_call" | custom-call | tf_op jit(solution)/shard_map/pallas_call | solution.py:384
  67.9 0.0 copy-start
  67.9 0.7 copy-done
  68.6 0.6 copy.8
  69.1 1.9 %copy.9 = f32[512,256]{1,0:T(8,128)} copy(f32[512,256]{1,0:T(8,128)} %get-tuple-element.9) | data formatting | bytes 1048576
Async XLA Ops:
  67.9 0.7 copy-start

commit v3 on v2

v3 whole, which is shorter than its diff:
```python
import functools
import math

import jax
import jax.numpy as jnp
from jax import lax
from jax.experimental import pallas as pl
from jax.experimental.pallas import tpu as pltpu
from jax.sharding import PartitionSpec as P

MESH = pl.DeviceIdType.MESH
F32 = jnp.float32
BF16 = jnp.bfloat16
LOWEST = -1e38


def kernel(sizes, src_hbm, tgt_hbm, pot_hbm, act_hbm, code_ref, note_ref,
           src, pot, act, local, held, scores, weights, crossed, top, rescale, total, turned, pairtop, pairturned, coded, mask, norm, stat,
           gotstat, gotnum, factor, recv, send_z, send_x, pair_recv, pair_send, rs_recv, rs_send, ag_recv, ag_send):
    nsrc, ntgt, eps = sizes
    rows, width = src_hbm.shape
    piece = tgt_hbm.shape[0] // 2
    block = 128
    rounds = ntgt // 4
    nz = ntgt // 4
    share = rows // nsrc
    sblocks = rows // block
    blocks = 2 * sblocks
    to_two = math.log2(math.e)

    s = lax.axis_index("src")
    t = lax.axis_index("tgt")
    half = nsrc // 2
    x_hi, y = s // half, s % half
    z, x_lo, core = t // 4, (t // 2) % 2, t % 2
    up = (s, (t + 4) % ntgt)
    down = (s, (t + ntgt - 4) % ntgt)
    twin = (s, z * 4 + x_lo * 2 + 1 - core)
    side_a = (s, z * 4 + (1 - x_lo) * 2 + core)
    side_b = ((1 - x_hi) * half + y, z * 4 + (1 - x_lo) * 2 + core)
    others = [((s + d) % nsrc, t) for d in range(1, nsrc)]

    barrier = pltpu.get_barrier_semaphore()
    for device in [up, down, twin, side_a, side_b] + others:
        pl.semaphore_signal(barrier, inc=1, device_id=device, device_id_type=MESH)

    loads = [
        pltpu.make_async_copy(tgt_hbm.at[part * piece + h * block:part * piece + (h + 1) * block, :],
                              held.at[0, 1 - part, h * (block + 16):h * (block + 16) + block, :], local.at[part, h])
        for part in range(2) for h in range(2)
    ] + [
        pltpu.make_async_copy(pot_hbm, pot, local.at[2, 0]),
        pltpu.make_async_copy(src_hbm, src.at[0:rows, :], local.at[2, 1]),
        pltpu.make_async_copy(act_hbm, act.at[0], local.at[3, 0]),
    ]
    for load in loads:
        load.start()

    def remote(source, target, ssem, rsem, device):
        return pltpu.make_async_remote_copy(
            src_ref=source, dst_ref=target, send_sem=ssem, recv_sem=rsem, device_id=device, device_id_type=MESH
        )

    parts_of = (slice(0, block + 16), slice(block + 16, 2 * block + 16))

    def send_up(k, lane, to, g):
        return remote(held.at[k, lane, parts_of[g], :], held.at[to, 0, parts_of[g], :],
                      send_z.at[0, to, g], recv.at[to, 0, g], up)

    def send_down(k, lane, to, g):
        return remote(held.at[k, lane, parts_of[g], :], held.at[to, 1, parts_of[g], :],
                      send_z.at[1, to, g], recv.at[to, 1, g], down)

    def send_a(k, lane, g):
        return remote(held.at[k, lane, parts_of[g], :], held.at[k, 2, parts_of[g], :],
                      send_x.at[0, k, g], recv.at[k, 2, g], side_a)

    def send_b(k, lane, g):
        return remote(held.at[k, lane, parts_of[g], :], held.at[k, 3, parts_of[g], :],
                      send_x.at[1, k, g], recv.at[k, 3, g], side_b)

    share_sources = remote(src_hbm, src.at[rows:2 * rows, :], pair_send.at[0, 0], pair_recv.at[0, 0], twin)
    share_active = remote(act_hbm, act.at[1], pair_send.at[1, 0], pair_recv.at[1, 0], twin)

    def arrived(k, lane, g):
        here = held.at[k, lane, parts_of[g], :]
        remote(here, here, send_z.at[0, 0, g], recv.at[k, lane, g], up).wait_recv()

    def points(k, lane):
        return jnp.concatenate([held[k, lane, 0:block, :], held[k, lane, block + 16:2 * block + 16, :]], axis=0)

    ones = jnp.ones((8, width), BF16)
    across = (((1,), (1,)), ((), ()))

    def half_norms(block_rows):
        wide = block_rows.astype(F32)
        square = 0.5 * (wide * wide)
        high = square.astype(BF16)
        low = (square - high.astype(F32)).astype(BF16)
        return lax.dot_general(ones, high, across, preferred_element_type=F32) + lax.dot_general(
            ones, low, across, preferred_element_type=F32
        )

    own_row = lax.broadcasted_iota(jnp.int32, (8, piece), 0) == lax.broadcasted_iota(jnp.int32, (8, piece), 1) % 8
    chooser = jnp.where(
        lax.broadcasted_iota(jnp.int32, (piece, block), 0) // 8 == lax.broadcasted_iota(jnp.int32, (piece, block), 1),
        1.0, 0.0,
    ).astype(BF16)

    for part in range(2):
        loads[2 * part].wait()
        loads[2 * part + 1].wait()
        if part == 0:
            loads[4].wait()
        data = points(0, 1 - part)
        shifted = (pot[0:1, part * piece:(part + 1) * piece] - half_norms(data)[0:1, :]) * (1.0 / eps)
        high = shifted.astype(BF16).astype(F32)
        middle = (shifted - high).astype(BF16).astype(F32)
        low = shifted - high - middle
        spread_out = [
            jnp.dot(jnp.where(own_row, jnp.broadcast_to(value, (8, piece)), 0.0).astype(BF16), chooser,
                    preferred_element_type=F32)
            for value in (high, middle, low)
        ]
        extra = jnp.concatenate([
            jnp.concatenate([spread_out[0], spread_out[1]], axis=1),
            jnp.concatenate([spread_out[2], jnp.zeros((8, block), F32)], axis=1),
        ], axis=0)
        held[0, 1 - part, block:block + 16, :] = extra.astype(BF16)

    pl.semaphore_wait(barrier, 5 + nsrc - 1)
    for g in range(2):
        send_up(0, 1, 1, g).start()
        send_down(0, 0, 1, g).start()
        send_a(0, 1, g).start()
        send_b(0, 0, g).start()
    share_sources.start()
    share_active.start()
    for g in range(2):
        send_up(0, 0, 2, g).start()
        send_down(0, 1, 2, g).start()

    loads[5].wait()
    loads[6].wait()

    for b in range(sblocks):
        norm[b:b + 1, :] = half_norms(src[b * block:(b + 1) * block, :])[0:1, :]

    slots = rounds * 4 * 2
    place = lax.broadcasted_iota(jnp.int32, (slots, block), 0)
    part_h, kind, k = place % 2, (place // 2) % 4, place // 8
    from_side = kind >= 2
    odd = k % 2
    distance = (k + 1) // 2
    below = jnp.where(kind == 0, 1, jnp.where(kind == 1, 0, jnp.where(kind == 2, odd, 1 - odd)))
    letter = jnp.where(kind == 0, 1 - odd, jnp.where(kind == 1, odd, kind - 2))
    z_from = (z + jnp.where(below == 1, nz - distance, distance)) % nz
    x_lo_from = jnp.where(from_side, 1 - x_lo, x_lo)
    x_hi_from = jnp.where(kind == 3, 1 - x_hi, x_hi)
    owner = (x_hi_from * half + y) * ntgt + z_from * 4 + x_lo_from * 2 + core
    number = owner * 4 + letter * 2 + part_h

    def set_mask(part):
        for b in range(sblocks):
            hit = jnp.zeros((slots, block), F32)
            for e in range(act.shape[2] // block):
                hit = jnp.where(number == act[part, b:b + 1, e * block:(e + 1) * block], 1.0, hit)
            mask[part * sblocks + b] = jnp.broadcast_to(jnp.max(hit, axis=1, keepdims=True), (slots, block))

    set_mask(0)
    top[...] = jnp.full(top.shape, LOWEST, F32)
    rescale[...] = jnp.ones(rescale.shape, F32)
    total[...] = jnp.zeros(total.shape, F32)
    turned[...] = jnp.zeros(turned.shape, F32)
    share_active.wait_recv()
    set_mask(1)
    share_sources.wait_recv()
    src[...] = (src[...].astype(F32) * (1.0 / eps)).astype(BF16)

    tile = scores.shape[2]
    per = block // 8

    def bit(k, lane, h, b):
        return mask[b, pl.ds((k * 4 + lane) * 2 + h, 1), :] > 0.5

    def score_piece(k, lane, n, maxima):
        product = lax.dot_general(
            points(k, lane), src[n * tile:(n + 1) * tile, :], across, preferred_element_type=F32
        )
        extra = held[k, lane, block:block + 16, :].astype(F32)
        shift = extra[0:8, 0:block] + extra[0:8, block:2 * block] + extra[8:16, 0:block]
        for h in range(piece // block):
            shifts = jnp.concatenate(
                [jnp.broadcast_to(shift[:, h * per + q:h * per + q + 1], (8, block)) for q in range(per)], axis=0
            )
            for c in range(tile // block):
                score = product[h * block:(h + 1) * block, c * block:(c + 1) * block] + shifts
                spot = lane * piece + h * block
                scores[n, spot:spot + block, c * block:(c + 1) * block] = score
                best = jnp.max(score.reshape(per, 8, block), axis=0)
                best = jnp.where(bit(k, lane, h, n * (tile // block) + c), best, LOWEST)
                maxima[c] = jnp.maximum(maxima[c], best)

    def weigh_piece(k, lane, n, tops, sums):
        for h in range(piece // block):
            for c in range(tile // block):
                spot = lane * piece + h * block
                against = jnp.where(bit(k, lane, h, n * (tile // block) + c), tops[c], -LOWEST)
                score = scores[n, spot:spot + block, c * block:(c + 1) * block]
                weight = jnp.exp2((score - against) * to_two)
                sums[c] = sums[c] + jnp.sum(weight.reshape(per, 8, block), axis=0)
                weights[n, spot:spot + block, c * block:(c + 1) * block] = weight.astype(BF16)

    def columns(n, c):
        return slice(n * tile + c * block, n * tile + (c + 1) * block)

    def absorb(fresh, ready, tick=None, fresh_lanes=(0, 1, 2, 3), ready_lanes=(0, 1, 2, 3), order=(0, 1, 2, 3), after=None):
        if ready is not None:
            for lane in ready_lanes:
                crossed[:, lane * piece:(lane + 1) * piece] = points(ready, lane).T
        parts = range(tile // block)
        for n in order:
            if tick is not None:
                tick(n)
            tops = [top[0:1, columns(n, c)] for c in parts]
            maxima = list(tops)
            scales = [rescale[0:1, columns(n, c)] for c in parts]
            sums = [total[:, columns(n, c)] * scales[c] for c in parts]
            added = None
            for lane in range(4):
                if ready is not None and lane in ready_lanes:
                    weigh_piece(ready, lane, n, tops, sums)
                if fresh is not None and lane in fresh_lanes:
                    score_piece(fresh, lane, n, maxima)
                if ready is not None and lane in ready_lanes and lane % 2 == 1:
                    span = slice((lane - 1) * piece, (lane + 1) * piece)
                    term = jnp.dot(crossed[:, span], weights[n, span, :], preferred_element_type=F32)
                    added = term if added is None else added + term
            for c in parts:
                at = columns(n, c)
                if ready is not None:
                    total[:, at] = sums[c]
                    turned[:, at] = turned[:, at] * scales[c] + added[:, c * block:(c + 1) * block]
                if fresh is not None:
                    new = jnp.max(maxima[c], axis=0, keepdims=True)
                    rescale[0:1, at] = jnp.exp2((tops[c] - new) * to_two)
                    top[0:1, at] = new
            if after is not None:
                after(n)

    def pass_on(k, lane, g):
        onward = (send_up, send_down)[lane]
        arrived(k, lane, g)

        @pl.when(k + 2 < rounds)
        def _():
            onward(k, lane, k + 2, g).start()

        @pl.when(k % 2 == 1 - lane)
        def _():
            send_a(k, lane, g).start()

        @pl.when(k % 2 == lane)
        def _():
            send_b(k, lane, g).start()

    def sides(k):
        for lane in (2, 3):
            for g in range(2):
                arrived(k, lane, g)

    def tick_of(k):
        def tick(n):
            if n % 2 == 0:
                for lane in range(2):
                    pass_on(k, lane, n // 2)
        return tick

    for g in range(2):
        for lane in range(2):
            pass_on(jnp.int32(1), lane, g)
    sides(0)
    absorb(0, None, tick_of(jnp.int32(2)))

    def one_round(k, carry):
        sides(k - 2)
        absorb(k - 2, k - 3, tick_of(k))
        return carry

    lax.fori_loop(3, rounds, one_round, 0)
    sides(rounds - 2)
    absorb(rounds - 2, rounds - 3)
    absorb(rounds - 1, rounds - 2, fresh_lanes=(0, 1))
    absorb(None, rounds - 1, ready_lanes=(0, 1))
    sides(rounds - 1)
    absorb(rounds - 1, None, fresh_lanes=(2, 3))

    def pair_copies(i):
        at = slice(rows + i * tile, rows + (i + 1) * tile)
        return (
            remote(top.at[:, at], pairtop.at[i], pair_send.at[2, i], pair_recv.at[2, i], twin),
            remote(turned.at[:, at], pairturned.at[i], pair_send.at[3, i], pair_recv.at[3, i], twin),
        )

    def share_of(q):
        return pl.ds(pl.multiple_of(q * share, share), share)

    def give_stat(q, d):
        return remote(stat.at[q // 2], gotstat.at[d], rs_send.at[0, d], rs_recv.at[0, d], (q, t))

    def give_rows(q, d):
        return remote(coded.at[share_of(q), :], gotnum.at[d], rs_send.at[1, d], rs_recv.at[1, d], (q, t))

    def merge(b):
        i, inside = b // (tile // block), slice(b % (tile // block) * block, (b % (tile // block) + 1) * block)
        at = slice(b * block, (b + 1) * block)
        best = jnp.maximum(top[0:1, at], pairtop[i, 0:1, inside])
        ours = jnp.exp2((top[0:1, at] - best) * to_two)
        theirs = jnp.exp2((pairtop[i, 0:1, inside] - best) * to_two)
        both = turned[:, at] * ours + pairturned[i, :, inside] * theirs
        largest = jnp.maximum(jnp.max(jnp.abs(both), axis=0, keepdims=True), 2e-38)
        stat[b, 0:1, :] = best
        stat[b, 1:2, :] = top[1:2, at] * ours + pairtop[i, 1:2, inside] * theirs
        stat[b, 2:3, :] = largest
        coded[at, :] = jnp.round((both * (1.0 / largest) * 32767.0).T).astype(jnp.int32).astype(jnp.int16)
        for q in (2 * b, 2 * b + 1):
            d = (q - s + nsrc) % nsrc

            @pl.when(q != s)
            def _():
                give_stat(q, d).start()
                give_rows(q, d).start()

    def after(n):
        for c in range(tile // block):
            at = columns(n, c)
            top[1:2, at] = jnp.sum(total[:, at], axis=0, keepdims=True)
        own = rows // tile
        if n >= own:
            for copy in pair_copies(n - own):
                copy.start()
        else:
            for copy in pair_copies(n):
                copy.wait_recv()
            for c in range(tile // block):
                merge(n * (tile // block) + c)

    absorb(None, rounds - 1, ready_lanes=(2, 3), order=(2, 3, 0, 1), after=after)

    gotstat[0] = stat[s // 2]
    mine = share_of(s)
    for d in range(1, nsrc):
        give_stat((s + d) % nsrc, d).wait_recv()
    tops = jnp.concatenate([gotstat[d, 0:1, :] for d in range(nsrc)], axis=0)
    dens = jnp.concatenate([gotstat[d, 1:2, :] for d in range(nsrc)], axis=0)
    sizes_of = jnp.concatenate([gotstat[d, 2:3, :] for d in range(nsrc)], axis=0)
    best = jnp.max(tops, axis=0, keepdims=True)
    scale = jnp.exp2((tops - best) * to_two)
    den = jnp.sum(scale * dens, axis=0, keepdims=True)
    value = norm[pl.ds(s // 2, 1), :] - eps * (best + jnp.log(den))
    ratio = scale / den * sizes_of
    bound = jnp.maximum(jnp.sum(ratio, axis=0, keepdims=True), 2e-38)
    note_ref[s] = jnp.concatenate([value, bound, jnp.zeros((6, block), F32)], axis=0)
    factor[...] = jnp.concatenate(
        [ratio, 1.0 / bound, jnp.zeros((block - nsrc - 1, block), F32)], axis=0
    ).T

    def spread_note(d):
        return remote(note_ref.at[s], note_ref.at[s], ag_send.at[0, d], ag_recv.at[0, d], ((s + d) % nsrc, t))

    def spread_rows(d):
        return remote(code_ref.at[mine, :], code_ref.at[mine, :], ag_send.at[1, d], ag_recv.at[1, d],
                      ((s + d) % nsrc, t))

    for d in range(1, nsrc):
        spread_note(d).start()
    column = factor[pl.ds(pl.multiple_of((s % 2) * share, share), share), :]

    def decoded(codes):
        return codes.astype(jnp.int32).astype(F32) * (1.0 / 32767.0)

    image = decoded(coded[mine, :]) * column[:, 0:1]
    for d in range(1, nsrc):
        give_rows((s + d) % nsrc, d).wait_recv()
        image = image + decoded(gotnum[d]) * column[:, d:d + 1]
    code_ref[mine, :] = jnp.round(image * column[:, nsrc:nsrc + 1] * 32767.0).astype(jnp.int32).astype(jnp.int16)

    for d in range(1, nsrc):
        spread_rows(d).start()

    for g in range(2):
        for to in (1, 2):
            send_up(0, 0, to, g).wait_send()
            send_down(0, 0, to, g).wait_send()
        send_a(0, 1, g).wait_send()
        send_b(0, 0, g).wait_send()

    def drain(k, carry):
        for g in range(2):
            @pl.when(k + 2 < rounds)
            def _():
                send_up(k, 0, k + 2, g).wait_send()
                send_down(k, 1, k + 2, g).wait_send()
            send_a(k, 0, g).wait_send()
            send_b(k, 0, g).wait_send()
        return carry

    lax.fori_loop(1, rounds, drain, 0)
    for copy in (share_sources, share_active) + pair_copies(0) + pair_copies(1):
        copy.wait_send()
    for d in range(1, nsrc):
        give_stat((s + d) % nsrc, d).wait_send()
        give_rows((s + d) % nsrc, d).wait_send()
    for d in range(1, nsrc):
        q = (s + nsrc - d) % nsrc
        remote(note_ref.at[q], note_ref.at[q], ag_send.at[0, d], ag_recv.at[0, d], (q, t)).wait_recv()
        remote(code_ref.at[share_of(q), :], code_ref.at[share_of(q), :], ag_send.at[1, d], ag_recv.at[1, d],
               (q, t)).wait_recv()
        spread_note(d).wait_send()
        spread_rows(d).wait_send()


def decode(share, code_ref, note_ref, val_ref, map_ref):
    block = 128
    lane = lax.broadcasted_iota(jnp.int32, (1, block), 1)
    blocks = range(val_ref.shape[0])
    bounds = []
    for b in blocks:
        first, second = note_ref[2 * b], note_ref[2 * b + 1]
        val_ref[b:b + 1, :] = jnp.where(lane < share, first[0:1, :], second[0:1, :])
        bounds.append(jnp.where(lane < share, first[1:2, :], second[1:2, :]))
    column = jnp.concatenate(bounds + [jnp.zeros((block - len(bounds), block), F32)], axis=0).T
    for b in blocks:
        at = slice(b * block, (b + 1) * block)
        map_ref[at, :] = code_ref[at, :].astype(jnp.int32).astype(F32) * (1.0 / 32767.0) * column[:, b:b + 1]


def per_device(sources, targets, target_potential, active):
    rows, width = sources.shape
    count = targets.shape[0]
    nsrc, ntgt = lax.axis_size("src"), lax.axis_size("tgt")
    eps = 0.5 * math.sqrt(width)
    piece = count // 2
    rounds = ntgt // 4
    share = rows // nsrc
    sblocks = rows // 128
    dma = pltpu.SemaphoreType.DMA
    vmem = pl.BlockSpec(memory_space=pltpu.VMEM)
    codes, notes = pl.pallas_call(
        functools.partial(kernel, (nsrc, ntgt, eps)),
        out_shape=(
            jax.ShapeDtypeStruct((rows, width), jnp.int16),
            jax.ShapeDtypeStruct((nsrc, 8, 128), F32),
        ),
        in_specs=[pl.BlockSpec(memory_space=pltpu.HBM)] * 4,
        out_specs=(vmem, vmem),
        scratch_shapes=[
            pltpu.VMEM((2 * rows, width), BF16),
            pltpu.VMEM((1, count), F32),
            pltpu.VMEM((2,) + active.shape, jnp.int32),
            dma((4, 2)),
            pltpu.VMEM((rounds, 4, piece + 16, width), BF16),
            pltpu.VMEM((2 * rows // 256, 4 * piece, 256), F32),
            pltpu.VMEM((2 * rows // 256, 4 * piece, 256), BF16),
            pltpu.VMEM((width, 4 * piece), BF16),
            pltpu.VMEM((8, 2 * rows), F32),
            pltpu.VMEM((8, 2 * rows), F32),
            pltpu.VMEM((8, 2 * rows), F32),
            pltpu.VMEM((width, 2 * rows), F32),
            pltpu.VMEM((rows // 256, 8, 256), F32),
            pltpu.VMEM((rows // 256, width, 256), F32),
            pltpu.VMEM((rows, width), jnp.int16),
            pltpu.VMEM((2 * sblocks, rounds * 8, 128), F32),
            pltpu.VMEM((sblocks, 128), F32),
            pltpu.VMEM((sblocks, 8, 128), F32),
            pltpu.VMEM((nsrc, 8, 128), F32),
            pltpu.VMEM((nsrc, share, width), jnp.int16),
            pltpu.VMEM((128, 128), F32),
            dma((rounds, 4, 2)),
            dma((2, rounds, 2)),
            dma((2, rounds, 2)),
            dma((4, 2)),
            dma((4, 2)),
            dma((2, nsrc)),
            dma((2, nsrc)),
            dma((2, nsrc)),
            dma((2, nsrc)),
        ],
        compiler_params=pltpu.CompilerParams(
            collective_id=0, has_side_effects=True, vmem_limit_bytes=56 * 1024 * 1024
        ),
    )(sources, targets, target_potential.reshape(1, count), active)
    value, image = pl.pallas_call(
        functools.partial(decode, share),
        out_shape=(
            jax.ShapeDtypeStruct((sblocks, 128), F32),
            jax.ShapeDtypeStruct((rows, width), F32),
        ),
        compiler_params=pltpu.CompilerParams(vmem_limit_bytes=60 * 1024 * 1024),
    )(codes, notes)
    return value.reshape(rows), image


def solution(mesh):
    return jax.shard_map(
        per_device,
        mesh=mesh,
        in_specs=(P("tgt", None), P(("src", "tgt"), None), P(("src", "tgt")), P("tgt", None)),
        out_specs=(P("tgt"), P("tgt", None)),
        check_vma=False,
    )
```

time: 71.2 us -> 60.9 us (0.86)
  Pallas kernels: 67.3 us -> 60.2 us
  local copies, waits for them, and re-layouts: 3.11 us -> 0 us
    pallas_call x1, Pallas kernels: 67.3 us -> 58.2 us  [per_device(): pl.pallas_call(functools.partial(kernel, (nsrc, ntgt, eps)), out_shape=(j...]
    unnamed x4 -> x0, local copies, waits for them, and re-layouts: 3.11 us -> none
    pallas_call x0 -> x1, Pallas kernels: none -> 2 us  [per_device(): pl.pallas_call(functools.partial(decode, share), out_shape=(jax.ShapeDtyp...]
where the time goes in v3:
time: 60.9 us; the launch traced here: 60.8 us
  Pallas kernels  60.2 us (99%)
  between operations  0.64 us (1%)
    pallas_call x1, Pallas kernels, per_device(): pl.pallas_call(functools.partial(kernel, (nsrc, ntgt, eps)), out_shape=(j...  58.2 us
    pallas_call x1, Pallas kernels, per_device(): pl.pallas_call(functools.partial(decode, share), out_shape=(jax.ShapeDtyp...  2 us

profile of v3, /device:TPU:1, one launch (start us, length us, event | category | flops | bytes accessed | tf_op | source)
XLA Modules:
  0.0 60.8 jit_solution(1008192859897974816)
XLA Ops:
  0.6 58.2 %shard_map.59 = (s16[512,256]{1,0:T(8,128)(2,1)}, f32[8,8,128]{2,1,0:T(8,128)}) custom-call(bf16[512,256]{1,0:T(8,128)(2,1)} %src_hbm.1, bf16[512,256]{1,0:T(8,128)(2,1)} %tgt_hbm.1, f32[1,512]{1,0:T(1,128)} %bitcast.2, s32[4,512]{1,0:T(4,128)} %act_hbm.1), custom_call_target="tpu_custom_call" | custom-call | tf_op jit(solution)/shard_map/pallas_call | solution.py:449
  58.8 2.0 %shard_map.60 = (f32[4,128]{1,0:T(4,128)}, f32[512,256]{1,0:T(8,128)}) custom-call(s16[512,256]{1,0:T(8,128)(2,1)} %get-tuple-element.6.code_ref, f32[8,8,128]{2,1,0:T(8,128)} %get-tuple-element.7.note_ref), custom_call_target="tpu_custom_call" | custom-call | tf_op jit(solution)/shard_map/pallas_call | solution.py:493

commit v4 on v3

--- a/solution.py
+++ b/solution.py
@@ -16,7 +16,7 @@
 
 def kernel(sizes, src_hbm, tgt_hbm, pot_hbm, act_hbm, code_ref, note_ref,
            src, pot, act, local, held, scores, weights, crossed, top, rescale, total, turned, pairtop, pairturned, coded, mask, norm, stat,
-           gotstat, gotnum, factor, recv, send_z, send_x, pair_recv, pair_send, rs_recv, rs_send, ag_recv, ag_send):
+           gotstat, gotnum, factor, recv, send_z, pair_recv, pair_send, end_recv, end_send, rs_recv, rs_send, ag_recv, ag_send):
     nsrc, ntgt, eps = sizes
     rows, width = src_hbm.shape
     piece = tgt_hbm.shape[0] // 2
@@ -25,7 +25,7 @@
     nz = ntgt // 4
     share = rows // nsrc
     sblocks = rows // block
-    blocks = 2 * sblocks
+    parts = 4
     to_two = math.log2(math.e)
 
     s = lax.axis_index("src")
@@ -38,10 +38,11 @@
     twin = (s, z * 4 + x_lo * 2 + 1 - core)
     side_a = (s, z * 4 + (1 - x_lo) * 2 + core)
     side_b = ((1 - x_hi) * half + y, z * 4 + (1 - x_lo) * 2 + core)
-    others = [((s + d) % nsrc, t) for d in range(1, nsrc)]
+    t_side = z * 4 + (1 - x_lo) * 2 + core
+    others = [((s + d) % nsrc, t) for d in range(1, nsrc)] + [((s + d) % nsrc, t_side) for d in range(nsrc)]
 
     barrier = pltpu.get_barrier_semaphore()
-    for device in [up, down, twin, side_a, side_b] + others:
+    for device in [up, down, twin] + others:
         pl.semaphore_signal(barrier, inc=1, device_id=device, device_id_type=MESH)
 
     loads = [
@@ -71,16 +72,17 @@
         return remote(held.at[k, lane, parts_of[g], :], held.at[to, 1, parts_of[g], :],
                       send_z.at[1, to, g], recv.at[to, 1, g], down)
 
-    def send_a(k, lane, g):
-        return remote(held.at[k, lane, parts_of[g], :], held.at[k, 2, parts_of[g], :],
-                      send_x.at[0, k, g], recv.at[k, 2, g], side_a)
-
-    def send_b(k, lane, g):
-        return remote(held.at[k, lane, parts_of[g], :], held.at[k, 3, parts_of[g], :],
-                      send_x.at[1, k, g], recv.at[k, 3, g], side_b)
-
-    share_sources = remote(src_hbm, src.at[rows:2 * rows, :], pair_send.at[0, 0], pair_recv.at[0, 0], twin)
-    share_active = remote(act_hbm, act.at[1], pair_send.at[1, 0], pair_recv.at[1, 0], twin)
+    def part_rows(part, g):
+        return src.at[part * rows + g * (rows // 2):part * rows + (g + 1) * (rows // 2), :]
+
+    def share_sources(part, g):
+        device = (twin, (side_a, side_b)[g], twin)[part - 1]
+        return remote(part_rows(2 if part == 3 else 0, g), part_rows(part, g),
+                      pair_send.at[part, g], pair_recv.at[part, g], device)
+
+    def share_active(part):
+        device = (twin, side_a, twin)[part - 1]
+        return remote(act.at[2 if part == 3 else 0], act.at[part], pair_send.at[part, 2], pair_recv.at[part, 2], device)
 
     def arrived(k, lane, g):
         here = held.at[k, lane, parts_of[g], :]
@@ -128,36 +130,33 @@
         ], axis=0)
         held[0, 1 - part, block:block + 16, :] = extra.astype(BF16)
 
-    pl.semaphore_wait(barrier, 5 + nsrc - 1)
+    loads[5].wait()
+    loads[6].wait()
+    for b in range(sblocks):
+        norm[b:b + 1, :] = half_norms(src[b * block:(b + 1) * block, :])[0:1, :]
+    src[0:rows, :] = (src[0:rows, :].astype(F32) * (1.0 / eps)).astype(BF16)
+
+    pl.semaphore_wait(barrier, 3 + 2 * nsrc - 1)
     for g in range(2):
         send_up(0, 1, 1, g).start()
         send_down(0, 0, 1, g).start()
-        send_a(0, 1, g).start()
-        send_b(0, 0, g).start()
-    share_sources.start()
-    share_active.start()
     for g in range(2):
+        share_sources(2, g).start()
+    share_active(2).start()
+    share_active(1).start()
+    for g in range(2):
+        share_sources(1, g).start()
         send_up(0, 0, 2, g).start()
         send_down(0, 1, 2, g).start()
 
-    loads[5].wait()
-    loads[6].wait()
-
-    for b in range(sblocks):
-        norm[b:b + 1, :] = half_norms(src[b * block:(b + 1) * block, :])[0:1, :]
-
-    slots = rounds * 4 * 2
+    slots = rounds * 2 * 2
     place = lax.broadcasted_iota(jnp.int32, (slots, block), 0)
-    part_h, kind, k = place % 2, (place // 2) % 4, place // 8
-    from_side = kind >= 2
+    part_h, kind, k = place % 2, (place // 2) % 2, place // 4
     odd = k % 2
     distance = (k + 1) // 2
-    below = jnp.where(kind == 0, 1, jnp.where(kind == 1, 0, jnp.where(kind == 2, odd, 1 - odd)))
-    letter = jnp.where(kind == 0, 1 - odd, jnp.where(kind == 1, odd, kind - 2))
-    z_from = (z + jnp.where(below == 1, nz - distance, distance)) % nz
-    x_lo_from = jnp.where(from_side, 1 - x_lo, x_lo)
-    x_hi_from = jnp.where(kind == 3, 1 - x_hi, x_hi)
-    owner = (x_hi_from * half + y) * ntgt + z_from * 4 + x_lo_from * 2 + core
+    letter = jnp.where(kind == 0, 1 - odd, odd)
+    z_from = (z + jnp.where(kind == 0, nz - distance, distance)) % nz
+    owner = (x_hi * half + y) * ntgt + z_from * 4 + x_lo * 2 + core
     number = owner * 4 + letter * 2 + part_h
 
     def set_mask(part):
@@ -172,16 +171,12 @@
     rescale[...] = jnp.ones(rescale.shape, F32)
     total[...] = jnp.zeros(total.shape, F32)
     turned[...] = jnp.zeros(turned.shape, F32)
-    share_active.wait_recv()
-    set_mask(1)
-    share_sources.wait_recv()
-    src[...] = (src[...].astype(F32) * (1.0 / eps)).astype(BF16)
 
     tile = scores.shape[2]
     per = block // 8
 
     def bit(k, lane, h, b):
-        return mask[b, pl.ds((k * 4 + lane) * 2 + h, 1), :] > 0.5
+        return mask[b, pl.ds((k * 2 + lane) * 2 + h, 1), :] > 0.5
 
     def score_piece(k, lane, n, maxima):
         product = lax.dot_general(
@@ -214,29 +209,28 @@
     def columns(n, c):
         return slice(n * tile + c * block, n * tile + (c + 1) * block)
 
-    def absorb(fresh, ready, tick=None, fresh_lanes=(0, 1, 2, 3), ready_lanes=(0, 1, 2, 3), order=(0, 1, 2, 3), after=None):
+    tiles = parts * rows // tile
+
+    def absorb(fresh, ready, tick=None, order=range(tiles), after=None):
         if ready is not None:
-            for lane in ready_lanes:
+            for lane in range(2):
                 crossed[:, lane * piece:(lane + 1) * piece] = points(ready, lane).T
-        parts = range(tile // block)
+        inside = range(tile // block)
         for n in order:
             if tick is not None:
                 tick(n)
-            tops = [top[0:1, columns(n, c)] for c in parts]
+            tops = [top[0:1, columns(n, c)] for c in inside]
             maxima = list(tops)
-            scales = [rescale[0:1, columns(n, c)] for c in parts]
-            sums = [total[:, columns(n, c)] * scales[c] for c in parts]
-            added = None
-            for lane in range(4):
-                if ready is not None and lane in ready_lanes:
+            scales = [rescale[0:1, columns(n, c)] for c in inside]
+            sums = [total[:, columns(n, c)] * scales[c] for c in inside]
+            for lane in range(2):
+                if ready is not None:
                     weigh_piece(ready, lane, n, tops, sums)
-                if fresh is not None and lane in fresh_lanes:
+                if fresh is not None:
                     score_piece(fresh, lane, n, maxima)
-                if ready is not None and lane in ready_lanes and lane % 2 == 1:
-                    span = slice((lane - 1) * piece, (lane + 1) * piece)
-                    term = jnp.dot(crossed[:, span], weights[n, span, :], preferred_element_type=F32)
-                    added = term if added is None else added + term
-            for c in parts:
+            if ready is not None:
+                added = jnp.dot(crossed[...], weights[n], preferred_element_type=F32)
+            for c in inside:
                 at = columns(n, c)
                 if ready is not None:
                     total[:, at] = sums[c]
@@ -256,104 +250,116 @@
         def _():
             onward(k, lane, k + 2, g).start()
 
-        @pl.when(k % 2 == 1 - lane)
-        def _():
-            send_a(k, lane, g).start()
-
-        @pl.when(k % 2 == lane)
-        def _():
-            send_b(k, lane, g).start()
-
-    def sides(k):
-        for lane in (2, 3):
-            for g in range(2):
-                arrived(k, lane, g)
-
     def tick_of(k):
         def tick(n):
-            if n % 2 == 0:
+            if n % (tiles // 2) == 0:
                 for lane in range(2):
-                    pass_on(k, lane, n // 2)
+                    pass_on(k, lane, n // (tiles // 2))
         return tick
 
+    share_active(2).wait_recv()
+    share_active(3).start()
+    for lane in range(2):
+        pass_on(jnp.int32(1), lane, 0)
     for g in range(2):
-        for lane in range(2):
-            pass_on(jnp.int32(1), lane, g)
-    sides(0)
+        share_sources(2, g).wait_recv()
+        share_sources(3, g).start()
+    for lane in range(2):
+        pass_on(jnp.int32(1), lane, 1)
+    share_active(1).wait_recv()
+    share_active(3).wait_recv()
+    for part in range(1, parts):
+        set_mask(part)
+    for part in (1, 3):
+        for g in range(2):
+            share_sources(part, g).wait_recv()
     absorb(0, None, tick_of(jnp.int32(2)))
 
     def one_round(k, carry):
-        sides(k - 2)
         absorb(k - 2, k - 3, tick_of(k))
         return carry
 
     lax.fori_loop(3, rounds, one_round, 0)
-    sides(rounds - 2)
     absorb(rounds - 2, rounds - 3)
-    absorb(rounds - 1, rounds - 2, fresh_lanes=(0, 1))
-    absorb(None, rounds - 1, ready_lanes=(0, 1))
-    sides(rounds - 1)
-    absorb(rounds - 1, None, fresh_lanes=(2, 3))
-
-    def pair_copies(i):
-        at = slice(rows + i * tile, rows + (i + 1) * tile)
+    absorb(rounds - 1, rounds - 2)
+
+    per_part = rows // tile
+
+    def pair_copies(part, i):
+        at = slice((part + 1) * rows + i * tile, (part + 1) * rows + (i + 1) * tile)
+        m = part // 2 * per_part + i
         return (
-            remote(top.at[:, at], pairtop.at[i], pair_send.at[2, i], pair_recv.at[2, i], twin),
-            remote(turned.at[:, at], pairturned.at[i], pair_send.at[3, i], pair_recv.at[3, i], twin),
+            remote(top.at[:, at], pairtop.at[m], end_send.at[0, m], end_recv.at[0, m], twin),
+            remote(turned.at[:, at], pairturned.at[m], end_send.at[1, m], end_recv.at[1, m], twin),
         )
 
     def share_of(q):
         return pl.ds(pl.multiple_of(q * share, share), share)
 
-    def give_stat(q, d):
-        return remote(stat.at[q // 2], gotstat.at[d], rs_send.at[0, d], rs_recv.at[0, d], (q, t))
-
-    def give_rows(q, d):
-        return remote(coded.at[share_of(q), :], gotnum.at[d], rs_send.at[1, d], rs_recv.at[1, d], (q, t))
-
-    def merge(b):
-        i, inside = b // (tile // block), slice(b % (tile // block) * block, (b % (tile // block) + 1) * block)
-        at = slice(b * block, (b + 1) * block)
-        best = jnp.maximum(top[0:1, at], pairtop[i, 0:1, inside])
+    def give_stat(part, q, d):
+        slot = d + part // 2 * nsrc
+        return remote(stat.at[part // 2 * sblocks + q // 2], gotstat.at[slot], rs_send.at[0, slot], rs_recv.at[0, slot],
+                      (q, t_side if part else t))
+
+    def give_rows(part, q, d):
+        slot = d + part // 2 * nsrc
+        return remote(coded.at[pl.ds(pl.multiple_of(part // 2 * rows + q * share, share), share), :], gotnum.at[slot],
+                      rs_send.at[1, slot], rs_recv.at[1, slot], (q, t_side if part else t))
+
+    def merge(part, b):
+        m, c = part // 2 * per_part + b // (tile // block), b % (tile // block)
+        inside = slice(c * block, (c + 1) * block)
+        at = slice(part * rows + b * block, part * rows + (b + 1) * block)
+        best = jnp.maximum(top[0:1, at], pairtop[m, 0:1, inside])
         ours = jnp.exp2((top[0:1, at] - best) * to_two)
-        theirs = jnp.exp2((pairtop[i, 0:1, inside] - best) * to_two)
-        both = turned[:, at] * ours + pairturned[i, :, inside] * theirs
+        theirs = jnp.exp2((pairtop[m, 0:1, inside] - best) * to_two)
+        both = turned[:, at] * ours + pairturned[m, :, inside] * theirs
         largest = jnp.maximum(jnp.max(jnp.abs(both), axis=0, keepdims=True), 2e-38)
-        stat[b, 0:1, :] = best
-        stat[b, 1:2, :] = top[1:2, at] * ours + pairtop[i, 1:2, inside] * theirs
-        stat[b, 2:3, :] = largest
-        coded[at, :] = jnp.round((both * (1.0 / largest) * 32767.0).T).astype(jnp.int32).astype(jnp.int16)
+        spot = part // 2 * sblocks + b
+        stat[spot, 0:1, :] = best
+        stat[spot, 1:2, :] = top[1:2, at] * ours + pairtop[m, 1:2, inside] * theirs
+        stat[spot, 2:3, :] = largest
+        coded[spot * block:(spot + 1) * block, :] = jnp.round(
+            (both * (1.0 / largest) * 32767.0).T
+        ).astype(jnp.int32).astype(jnp.int16)
         for q in (2 * b, 2 * b + 1):
             d = (q - s + nsrc) % nsrc
-
-            @pl.when(q != s)
-            def _():
-                give_stat(q, d).start()
-                give_rows(q, d).start()
+            if part:
+                give_stat(part, q, d).start()
+                give_rows(part, q, d).start()
+            else:
+                @pl.when(q != s)
+                def _():
+                    give_stat(part, q, d).start()
+                    give_rows(part, q, d).start()
 
     def after(n):
+        part, i = n // per_part, n % per_part
         for c in range(tile // block):
             at = columns(n, c)
             top[1:2, at] = jnp.sum(total[:, at], axis=0, keepdims=True)
-        own = rows // tile
-        if n >= own:
-            for copy in pair_copies(n - own):
+        if part % 2 == 1:
+            for copy in pair_copies(part - 1, i):
                 copy.start()
         else:
-            for copy in pair_copies(n):
+            for copy in pair_copies(part, i):
                 copy.wait_recv()
             for c in range(tile // block):
-                merge(n * (tile // block) + c)
-
-    absorb(None, rounds - 1, ready_lanes=(2, 3), order=(2, 3, 0, 1), after=after)
+                merge(part, i * (tile // block) + c)
+
+    order = [part * per_part + i for part in (3, 1, 2, 0) for i in range(per_part)]
+    absorb(None, rounds - 1, order=order, after=after)
 
     gotstat[0] = stat[s // 2]
     mine = share_of(s)
     for d in range(1, nsrc):
-        give_stat((s + d) % nsrc, d).wait_recv()
-    tops = jnp.concatenate([gotstat[d, 0:1, :] for d in range(nsrc)], axis=0)
-    dens = jnp.concatenate([gotstat[d, 1:2, :] for d in range(nsrc)], axis=0)
-    sizes_of = jnp.concatenate([gotstat[d, 2:3, :] for d in range(nsrc)], axis=0)
+        give_stat(0, (s + d) % nsrc, d).wait_recv()
+    for d in range(nsrc):
+        give_stat(2, (s + d) % nsrc, d).wait_recv()
+    slots = range(2 * nsrc)
+    tops = jnp.concatenate([gotstat[d, 0:1, :] for d in slots], axis=0)
+    dens = jnp.concatenate([gotstat[d, 1:2, :] for d in slots], axis=0)
+    sizes_of = jnp.concatenate([gotstat[d, 2:3, :] for d in slots], axis=0)
     best = jnp.max(tops, axis=0, keepdims=True)
     scale = jnp.exp2((tops - best) * to_two)
     den = jnp.sum(scale * dens, axis=0, keepdims=True)
@@ -362,7 +368,7 @@
     bound = jnp.maximum(jnp.sum(ratio, axis=0, keepdims=True), 2e-38)
     note_ref[s] = jnp.concatenate([value, bound, jnp.zeros((6, block), F32)], axis=0)
     factor[...] = jnp.concatenate(
-        [ratio, 1.0 / bound, jnp.zeros((block - nsrc - 1, block), F32)], axis=0
+        [ratio, 1.0 / bound, jnp.zeros((block - 2 * nsrc - 1, block), F32)], axis=0
     ).T
 
     def spread_note(d):
@@ -380,10 +386,10 @@
         return codes.astype(jnp.int32).astype(F32) * (1.0 / 32767.0)
 
     image = decoded(coded[mine, :]) * column[:, 0:1]
-    for d in range(1, nsrc):
-        give_rows((s + d) % nsrc, d).wait_recv()
-        image = image + decoded(gotnum[d]) * column[:, d:d + 1]
-    code_ref[mine, :] = jnp.round(image * column[:, nsrc:nsrc + 1] * 32767.0).astype(jnp.int32).astype(jnp.int16)
+    for slot in [nsrc + d for d in range(nsrc)] + list(range(1, nsrc)):
+        give_rows(slot // nsrc * 2, (s + slot) % nsrc, slot % nsrc).wait_recv()
+        image = image + decoded(gotnum[slot]) * column[:, slot:slot + 1]
+    code_ref[mine, :] = jnp.round(image * column[:, 2 * nsrc:2 * nsrc + 1] * 32767.0).astype(jnp.int32).astype(jnp.int16)
 
     for d in range(1, nsrc):
         spread_rows(d).start()
@@ -392,8 +398,6 @@
         for to in (1, 2):
             send_up(0, 0, to, g).wait_send()
             send_down(0, 0, to, g).wait_send()
-        send_a(0, 1, g).wait_send()
-        send_b(0, 0, g).wait_send()
 
     def drain(k, carry):
         for g in range(2):
@@ -401,16 +405,23 @@
             def _():
                 send_up(k, 0, k + 2, g).wait_send()
                 send_down(k, 1, k + 2, g).wait_send()
-            send_a(k, 0, g).wait_send()
-            send_b(k, 0, g).wait_send()
         return carry
 
     lax.fori_loop(1, rounds, drain, 0)
-    for copy in (share_sources, share_active) + pair_copies(0) + pair_copies(1):
-        copy.wait_send()
+    for part in range(1, parts):
+        share_active(part).wait_send()
+        for g in range(2):
+            share_sources(part, g).wait_send()
+    for part in (0, 2):
+        for i in range(per_part):
+            for copy in pair_copies(part, i):
+                copy.wait_send()
     for d in range(1, nsrc):
-        give_stat((s + d) % nsrc, d).wait_send()
-        give_rows((s + d) % nsrc, d).wait_send()
+        give_stat(0, (s + d) % nsrc, d).wait_send()
+        give_rows(0, (s + d) % nsrc, d).wait_send()
+    for d in range(nsrc):
+        give_stat(2, (s + d) % nsrc, d).wait_send()
+        give_rows(2, (s + d) % nsrc, d).wait_send()
     for d in range(1, nsrc):
         q = (s + nsrc - d) % nsrc
         remote(note_ref.at[q], note_ref.at[q], ag_send.at[0, d], ag_recv.at[0, d], (q, t)).wait_recv()
@@ -455,34 +466,35 @@
         in_specs=[pl.BlockSpec(memory_space=pltpu.HBM)] * 4,
         out_specs=(vmem, vmem),
         scratch_shapes=[
-            pltpu.VMEM((2 * rows, width), BF16),
+            pltpu.VMEM((4 * rows, width), BF16),
             pltpu.VMEM((1, count), F32),
-            pltpu.VMEM((2,) + active.shape, jnp.int32),
+            pltpu.VMEM((4,) + active.shape, jnp.int32),
             dma((4, 2)),
-            pltpu.VMEM((rounds, 4, piece + 16, width), BF16),
-            pltpu.VMEM((2 * rows // 256, 4 * piece, 256), F32),
-            pltpu.VMEM((2 * rows // 256, 4 * piece, 256), BF16),
-            pltpu.VMEM((width, 4 * piece), BF16),
-            pltpu.VMEM((8, 2 * rows), F32),
-            pltpu.VMEM((8, 2 * rows), F32),
-            pltpu.VMEM((8, 2 * rows), F32),
-            pltpu.VMEM((width, 2 * rows), F32),
-            pltpu.VMEM((rows // 256, 8, 256), F32),
-            pltpu.VMEM((rows // 256, width, 256), F32),
-            pltpu.VMEM((rows, width), jnp.int16),
-            pltpu.VMEM((2 * sblocks, rounds * 8, 128), F32),
+            pltpu.VMEM((rounds, 2, piece + 16, width), BF16),
+            pltpu.VMEM((4 * rows // 256, 2 * piece, 256), F32),
+            pltpu.VMEM((4 * rows // 256, 2 * piece, 256), BF16),
+            pltpu.VMEM((width, 2 * piece), BF16),
+            pltpu.VMEM((8, 4 * rows), F32),
+            pltpu.VMEM((8, 4 * rows), F32),
+            pltpu.VMEM((8, 4 * rows), F32),
+            pltpu.VMEM((width, 4 * rows), F32),
+            pltpu.VMEM((2 * rows // 256, 8, 256), F32),
+            pltpu.VMEM((2 * rows // 256, width, 256), F32),
+            pltpu.VMEM((2 * rows, width), jnp.int16),
+            pltpu.VMEM((4 * sblocks, rounds * 4, 128), F32),
             pltpu.VMEM((sblocks, 128), F32),
-            pltpu.VMEM((sblocks, 8, 128), F32),
-            pltpu.VMEM((nsrc, 8, 128), F32),
-            pltpu.VMEM((nsrc, share, width), jnp.int16),
+            pltpu.VMEM((2 * sblocks, 8, 128), F32),
+            pltpu.VMEM((2 * nsrc, 8, 128), F32),
+            pltpu.VMEM((2 * nsrc, share, width), jnp.int16),
             pltpu.VMEM((128, 128), F32),
-            dma((rounds, 4, 2)),
+            dma((rounds, 2, 2)),
             dma((2, rounds, 2)),
-            dma((2, rounds, 2)),
-            dma((4, 2)),
-            dma((4, 2)),
-            dma((2, nsrc)),
-            dma((2, nsrc)),
+            dma((4, 3)),
+            dma((4, 3)),
+            dma((2, 2 * rows // 256)),
+            dma((2, 2 * rows // 256)),
+            dma((2, 2 * nsrc)),
+            dma((2, 2 * nsrc)),
             dma((2, nsrc)),
             dma((2, nsrc)),
         ],

time: 60.9 us -> 61.8 us (1.015)
  Pallas kernels: 60.2 us -> 60.9 us
    pallas_call x1, Pallas kernels: 58.2 us -> 58.9 us  [per_device(): pl.pallas_call(functools.partial(kernel, (nsrc, ntgt, eps)), out_shape=(j...]
where the time goes in v4:
time: 61.8 us; the launch traced here: 61.5 us
  Pallas kernels  60.9 us (99%)
  between operations  0.64 us (1%)
    pallas_call x1, Pallas kernels, per_device(): pl.pallas_call(functools.partial(kernel, (nsrc, ntgt, eps)), out_shape=(j...  58.9 us
    pallas_call x1, Pallas kernels, per_device(): pl.pallas_call(functools.partial(decode, share), out_shape=(jax.ShapeDtyp...  2 us

profile of v4, /device:TPU:1, one launch (start us, length us, event | category | flops | bytes accessed | tf_op | source)
XLA Modules:
  0.0 61.5 jit_solution(9223441709216587517)
XLA Ops:
  0.6 58.9 %shard_map.59 = (s16[512,256]{1,0:T(8,128)(2,1)}, f32[8,8,128]{2,1,0:T(8,128)}) custom-call(bf16[512,256]{1,0:T(8,128)(2,1)} %src_hbm.1, bf16[512,256]{1,0:T(8,128)(2,1)} %tgt_hbm.1, f32[1,512]{1,0:T(1,128)} %bitcast.2, s32[4,512]{1,0:T(4,128)} %act_hbm.1), custom_call_target="tpu_custom_call" | custom-call | tf_op jit(solution)/shard_map/pallas_call | solution.py:460
  59.5 2.0 %shard_map.60 = (f32[4,128]{1,0:T(4,128)}, f32[512,256]{1,0:T(8,128)}) custom-call(s16[512,256]{1,0:T(8,128)(2,1)} %get-tuple-element.6.code_ref, f32[8,8,128]{2,1,0:T(8,128)} %get-tuple-element.7.note_ref), custom_call_target="tpu_custom_call" | custom-call | tf_op jit(solution)/shard_map/pallas_call | solution.py:505

commit v5 on v4

--- a/solution.py
+++ b/solution.py
@@ -12,6 +12,7 @@
 F32 = jnp.float32
 BF16 = jnp.bfloat16
 LOWEST = -1e38
+TILE = 512
 
 
 def kernel(sizes, src_hbm, tgt_hbm, pot_hbm, act_hbm, code_ref, note_ref,
@@ -471,15 +472,15 @@
             pltpu.VMEM((4,) + active.shape, jnp.int32),
             dma((4, 2)),
             pltpu.VMEM((rounds, 2, piece + 16, width), BF16),
-            pltpu.VMEM((4 * rows // 256, 2 * piece, 256), F32),
-            pltpu.VMEM((4 * rows // 256, 2 * piece, 256), BF16),
+            pltpu.VMEM((4 * rows // TILE, 2 * piece, TILE), F32),
+            pltpu.VMEM((4 * rows // TILE, 2 * piece, TILE), BF16),
             pltpu.VMEM((width, 2 * piece), BF16),
             pltpu.VMEM((8, 4 * rows), F32),
             pltpu.VMEM((8, 4 * rows), F32),
             pltpu.VMEM((8, 4 * rows), F32),
             pltpu.VMEM((width, 4 * rows), F32),
-            pltpu.VMEM((2 * rows // 256, 8, 256), F32),
-            pltpu.VMEM((2 * rows // 256, width, 256), F32),
+            pltpu.VMEM((2 * rows // TILE, 8, TILE), F32),
+            pltpu.VMEM((2 * rows // TILE, width, TILE), F32),
             pltpu.VMEM((2 * rows, width), jnp.int16),
             pltpu.VMEM((4 * sblocks, rounds * 4, 128), F32),
             pltpu.VMEM((sblocks, 128), F32),
@@ -491,8 +492,8 @@
             dma((2, rounds, 2)),
             dma((4, 3)),
             dma((4, 3)),
-            dma((2, 2 * rows // 256)),
-            dma((2, 2 * rows // 256)),
+            dma((2, 2 * rows // TILE)),
+            dma((2, 2 * rows // TILE)),
             dma((2, 2 * nsrc)),
             dma((2, 2 * nsrc)),
             dma((2, nsrc)),

time: 61.8 us -> 63.3 us (1.024)
  Pallas kernels: 60.9 us -> 62.6 us
    pallas_call x1, Pallas kernels: 58.9 us -> 60.6 us  [per_device(): pl.pallas_call(functools.partial(kernel, (nsrc, ntgt, eps)), out_shape=(j...]
where the time goes in v5:
time: 63.3 us; the launch traced here: 63.2 us
  Pallas kernels  62.6 us (99%)
  between operations  0.64 us (1%)
    pallas_call x1, Pallas kernels, per_device(): pl.pallas_call(functools.partial(kernel, (nsrc, ntgt, eps)), out_shape=(j...  60.6 us
    pallas_call x1, Pallas kernels, per_device(): pl.pallas_call(functools.partial(decode, share), out_shape=(jax.ShapeDtyp...  2 us

profile of v5, /device:TPU:1, one launch (start us, length us, event | category | flops | bytes accessed | tf_op | source)
XLA Modules:
  0.0 63.2 jit_solution(12431025896277804156)
XLA Ops:
  0.6 60.6 %shard_map.59 = (s16[512,256]{1,0:T(8,128)(2,1)}, f32[8,8,128]{2,1,0:T(8,128)}) custom-call(bf16[512,256]{1,0:T(8,128)(2,1)} %src_hbm.1, bf16[512,256]{1,0:T(8,128)(2,1)} %tgt_hbm.1, f32[1,512]{1,0:T(1,128)} %bitcast.2, s32[4,512]{1,0:T(4,128)} %act_hbm.1), custom_call_target="tpu_custom_call" | custom-call | tf_op jit(solution)/shard_map/pallas_call | solution.py:461
  61.2 2.0 %shard_map.60 = (f32[4,128]{1,0:T(4,128)}, f32[512,256]{1,0:T(8,128)}) custom-call(s16[512,256]{1,0:T(8,128)(2,1)} %get-tuple-element.6.code_ref, f32[8,8,128]{2,1,0:T(8,128)} %get-tuple-element.7.note_ref), custom_call_target="tpu_custom_call" | custom-call | tf_op jit(solution)/shard_map/pallas_call | solution.py:506

commit v6 on v3

--- a/solution.py
+++ b/solution.py
@@ -15,7 +15,7 @@
 
 
 def kernel(sizes, src_hbm, tgt_hbm, pot_hbm, act_hbm, code_ref, note_ref,
-           src, pot, act, local, held, scores, weights, crossed, top, rescale, total, turned, pairtop, pairturned, coded, mask, norm, stat,
+           src, pot, act, local, held, scores, weights, crossed, spread, top, rescale, total, turned, pairtop, pairturned, coded, mask, norm, stat,
            gotstat, gotnum, factor, recv, send_z, send_x, pair_recv, pair_send, rs_recv, rs_send, ag_recv, ag_send):
     nsrc, ntgt, eps = sizes
     rows, width = src_hbm.shape
@@ -72,12 +72,12 @@
                       send_z.at[1, to, g], recv.at[to, 1, g], down)
 
     def send_a(k, lane, g):
-        return remote(held.at[k, lane, parts_of[g], :], held.at[k, 2, parts_of[g], :],
-                      send_x.at[0, k, g], recv.at[k, 2, g], side_a)
+        return remote(held.at[k, lane, parts_of[g], :], held.at[k + 1, 2, parts_of[g], :],
+                      send_x.at[0, k, g], recv.at[k + 1, 2, g], side_a)
 
     def send_b(k, lane, g):
-        return remote(held.at[k, lane, parts_of[g], :], held.at[k, 3, parts_of[g], :],
-                      send_x.at[1, k, g], recv.at[k, 3, g], side_b)
+        return remote(held.at[k, lane, parts_of[g], :], held.at[k + 1, 3, parts_of[g], :],
+                      send_x.at[1, k, g], recv.at[k + 1, 3, g], side_b)
 
     share_sources = remote(src_hbm, src.at[rows:2 * rows, :], pair_send.at[0, 0], pair_recv.at[0, 0], twin)
     share_active = remote(act_hbm, act.at[1], pair_send.at[1, 0], pair_recv.at[1, 0], twin)
@@ -136,9 +136,6 @@
         send_b(0, 0, g).start()
     share_sources.start()
     share_active.start()
-    for g in range(2):
-        send_up(0, 0, 2, g).start()
-        send_down(0, 1, 2, g).start()
 
     loads[5].wait()
     loads[6].wait()
@@ -146,10 +143,11 @@
     for b in range(sblocks):
         norm[b:b + 1, :] = half_norms(src[b * block:(b + 1) * block, :])[0:1, :]
 
-    slots = rounds * 4 * 2
+    slots = (rounds + 1) * 4 * 2
     place = lax.broadcasted_iota(jnp.int32, (slots, block), 0)
     part_h, kind, k = place % 2, (place // 2) % 4, place // 8
     from_side = kind >= 2
+    k = jnp.where(from_side, k - 1, k)
     odd = k % 2
     distance = (k + 1) // 2
     below = jnp.where(kind == 0, 1, jnp.where(kind == 1, 0, jnp.where(kind == 2, odd, 1 - odd)))
@@ -172,6 +170,11 @@
     rescale[...] = jnp.ones(rescale.shape, F32)
     total[...] = jnp.zeros(total.shape, F32)
     turned[...] = jnp.zeros(turned.shape, F32)
+    for g in range(2):
+        send_up(0, 1, 1, g).wait_send()
+        send_up(0, 0, 2, g).start()
+        send_down(0, 0, 1, g).wait_send()
+        send_down(0, 1, 2, g).start()
     share_active.wait_recv()
     set_mask(1)
     share_sources.wait_recv()
@@ -187,12 +190,8 @@
         product = lax.dot_general(
             points(k, lane), src[n * tile:(n + 1) * tile, :], across, preferred_element_type=F32
         )
-        extra = held[k, lane, block:block + 16, :].astype(F32)
-        shift = extra[0:8, 0:block] + extra[0:8, block:2 * block] + extra[8:16, 0:block]
         for h in range(piece // block):
-            shifts = jnp.concatenate(
-                [jnp.broadcast_to(shift[:, h * per + q:h * per + q + 1], (8, block)) for q in range(per)], axis=0
-            )
+            shifts = spread[lane * piece + h * block:lane * piece + (h + 1) * block, :]
             for c in range(tile // block):
                 score = product[h * block:(h + 1) * block, c * block:(c + 1) * block] + shifts
                 spot = lane * piece + h * block
@@ -200,6 +199,12 @@
                 best = jnp.max(score.reshape(per, 8, block), axis=0)
                 best = jnp.where(bit(k, lane, h, n * (tile // block) + c), best, LOWEST)
                 maxima[c] = jnp.maximum(maxima[c], best)
+
+    def spread_shifts(k, lane):
+        extra = held[k, lane, block:block + 16, :].astype(F32)
+        shift = extra[0:8, 0:block] + extra[0:8, block:2 * block] + extra[8:16, 0:block]
+        for q in range(piece // 8):
+            spread[lane * piece + 8 * q:lane * piece + 8 * q + 8, :] = jnp.broadcast_to(shift[:, q:q + 1], (8, block))
 
     def weigh_piece(k, lane, n, tops, sums):
         for h in range(piece // block):
@@ -214,12 +219,20 @@
     def columns(n, c):
         return slice(n * tile + c * block, n * tile + (c + 1) * block)
 
-    def absorb(fresh, ready, tick=None, fresh_lanes=(0, 1, 2, 3), ready_lanes=(0, 1, 2, 3), order=(0, 1, 2, 3), after=None):
+    everything = (0, 1, 2, 3)
+
+    def cross(k, lanes):
+        for lane in lanes:
+            crossed[:, lane * piece:(lane + 1) * piece] = points(k, lane).T
+
+    def absorb(fresh, ready, tick=None, fresh_lanes=everything, ready_lanes=everything):
         if ready is not None:
-            for lane in ready_lanes:
-                crossed[:, lane * piece:(lane + 1) * piece] = points(ready, lane).T
+            cross(ready, ready_lanes)
+        if fresh is not None:
+            for lane in fresh_lanes:
+                spread_shifts(fresh, lane)
         parts = range(tile // block)
-        for n in order:
+        for n in range(2 * rows // tile):
             if tick is not None:
                 tick(n)
             tops = [top[0:1, columns(n, c)] for c in parts]
@@ -245,8 +258,30 @@
                     new = jnp.max(maxima[c], axis=0, keepdims=True)
                     rescale[0:1, at] = jnp.exp2((tops[c] - new) * to_two)
                     top[0:1, at] = new
-            if after is not None:
-                after(n)
+
+    def finish(k, after):
+        cross(k, (2, 3))
+        for lane in (2, 3):
+            spread_shifts(k, lane)
+        parts = range(tile // block)
+        span = slice(2 * piece, 4 * piece)
+        for n in (2, 3, 0, 1):
+            tops = [top[0:1, columns(n, c)] for c in parts]
+            maxima = list(tops)
+            for lane in (2, 3):
+                score_piece(k, lane, n, maxima)
+            new = [jnp.max(maxima[c], axis=0, keepdims=True) for c in parts]
+            scales = [jnp.exp2((tops[c] - new[c]) * to_two) for c in parts]
+            sums = [total[:, columns(n, c)] * scales[c] for c in parts]
+            for lane in (2, 3):
+                weigh_piece(k, lane, n, new, sums)
+            added = jnp.dot(crossed[:, span], weights[n, span, :], preferred_element_type=F32)
+            for c in parts:
+                at = columns(n, c)
+                top[0:1, at] = new[c]
+                top[1:2, at] = jnp.sum(sums[c], axis=0, keepdims=True)
+                turned[:, at] = turned[:, at] * scales[c] + added[:, c * block:(c + 1) * block]
+            after(n)
 
     def pass_on(k, lane, g):
         onward = (send_up, send_down)[lane]
@@ -276,24 +311,20 @@
                     pass_on(k, lane, n // 2)
         return tick
 
-    for g in range(2):
-        for lane in range(2):
-            pass_on(jnp.int32(1), lane, g)
-    sides(0)
-    absorb(0, None, tick_of(jnp.int32(2)))
+    absorb(0, None, tick_of(jnp.int32(1)), fresh_lanes=(0, 1))
+    sides(1)
+    absorb(1, 0, tick_of(jnp.int32(2)), ready_lanes=(0, 1))
 
     def one_round(k, carry):
-        sides(k - 2)
-        absorb(k - 2, k - 3, tick_of(k))
+        sides(k - 1)
+        absorb(k - 1, k - 2, tick_of(k))
         return carry
 
     lax.fori_loop(3, rounds, one_round, 0)
-    sides(rounds - 2)
-    absorb(rounds - 2, rounds - 3)
-    absorb(rounds - 1, rounds - 2, fresh_lanes=(0, 1))
-    absorb(None, rounds - 1, ready_lanes=(0, 1))
     sides(rounds - 1)
-    absorb(rounds - 1, None, fresh_lanes=(2, 3))
+    absorb(rounds - 1, rounds - 2)
+    absorb(None, rounds - 1)
+    sides(rounds)
 
     def pair_copies(i):
         at = slice(rows + i * tile, rows + (i + 1) * tile)
@@ -332,9 +363,6 @@
                 give_rows(q, d).start()
 
     def after(n):
-        for c in range(tile // block):
-            at = columns(n, c)
-            top[1:2, at] = jnp.sum(total[:, at], axis=0, keepdims=True)
         own = rows // tile
         if n >= own:
             for copy in pair_copies(n - own):
@@ -345,7 +373,7 @@
             for c in range(tile // block):
                 merge(n * (tile // block) + c)
 
-    absorb(None, rounds - 1, ready_lanes=(2, 3), order=(2, 3, 0, 1), after=after)
+    finish(rounds, after)
 
     gotstat[0] = stat[s // 2]
     mine = share_of(s)
@@ -389,9 +417,8 @@
         spread_rows(d).start()
 
     for g in range(2):
-        for to in (1, 2):
-            send_up(0, 0, to, g).wait_send()
-            send_down(0, 0, to, g).wait_send()
+        send_up(0, 0, 2, g).wait_send()
+        send_down(0, 1, 2, g).wait_send()
         send_a(0, 1, g).wait_send()
         send_b(0, 0, g).wait_send()
 
@@ -423,16 +450,16 @@
 def decode(share, code_ref, note_ref, val_ref, map_ref):
     block = 128
     lane = lax.broadcasted_iota(jnp.int32, (1, block), 1)
-    blocks = range(val_ref.shape[0])
-    bounds = []
-    for b in blocks:
-        first, second = note_ref[2 * b], note_ref[2 * b + 1]
-        val_ref[b:b + 1, :] = jnp.where(lane < share, first[0:1, :], second[0:1, :])
-        bounds.append(jnp.where(lane < share, first[1:2, :], second[1:2, :]))
-    column = jnp.concatenate(bounds + [jnp.zeros((block - len(bounds), block), F32)], axis=0).T
-    for b in blocks:
-        at = slice(b * block, (b + 1) * block)
-        map_ref[at, :] = code_ref[at, :].astype(jnp.int32).astype(F32) * (1.0 / 32767.0) * column[:, b:b + 1]
+    b = pl.program_id(0)
+
+    @pl.when(b == 0)
+    def _():
+        for at in range(val_ref.shape[0]):
+            val_ref[at:at + 1, :] = jnp.where(lane < share, note_ref[2 * at, 0:1, :], note_ref[2 * at + 1, 0:1, :])
+
+    bound = jnp.where(lane < share, note_ref[2 * b, 1:2, :], note_ref[2 * b + 1, 1:2, :])
+    column = jnp.broadcast_to(bound, (block, block)).T
+    map_ref[...] = code_ref[...].astype(jnp.int32).astype(F32) * (1.0 / 32767.0) * column[:, 0:1]
 
 
 def per_device(sources, targets, target_potential, active):
@@ -459,10 +486,11 @@
             pltpu.VMEM((1, count), F32),
             pltpu.VMEM((2,) + active.shape, jnp.int32),
             dma((4, 2)),
-            pltpu.VMEM((rounds, 4, piece + 16, width), BF16),
+            pltpu.VMEM((rounds + 1, 4, piece + 16, width), BF16),
             pltpu.VMEM((2 * rows // 256, 4 * piece, 256), F32),
             pltpu.VMEM((2 * rows // 256, 4 * piece, 256), BF16),
             pltpu.VMEM((width, 4 * piece), BF16),
+            pltpu.VMEM((4 * piece, 128), F32),
             pltpu.VMEM((8, 2 * rows), F32),
             pltpu.VMEM((8, 2 * rows), F32),
             pltpu.VMEM((8, 2 * rows), F32),
@@ -470,13 +498,13 @@
             pltpu.VMEM((rows // 256, 8, 256), F32),
             pltpu.VMEM((rows // 256, width, 256), F32),
             pltpu.VMEM((rows, width), jnp.int16),
-            pltpu.VMEM((2 * sblocks, rounds * 8, 128), F32),
+            pltpu.VMEM((2 * sblocks, (rounds + 1) * 8, 128), F32),
             pltpu.VMEM((sblocks, 128), F32),
             pltpu.VMEM((sblocks, 8, 128), F32),
             pltpu.VMEM((nsrc, 8, 128), F32),
             pltpu.VMEM((nsrc, share, width), jnp.int16),
             pltpu.VMEM((128, 128), F32),
-            dma((rounds, 4, 2)),
+            dma((rounds + 1, 4, 2)),
             dma((2, rounds, 2)),
             dma((2, rounds, 2)),
             dma((4, 2)),
@@ -496,6 +524,15 @@
             jax.ShapeDtypeStruct((sblocks, 128), F32),
             jax.ShapeDtypeStruct((rows, width), F32),
         ),
+        grid=(sblocks,),
+        in_specs=[
+            pl.BlockSpec((128, width), lambda b: (b, 0)),
+            pl.BlockSpec((nsrc, 8, 128), lambda b: (0, 0, 0)),
+        ],
+        out_specs=(
+            pl.BlockSpec((sblocks, 128), lambda b: (0, 0)),
+            pl.BlockSpec((128, width), lambda b: (b, 0)),
+        ),
         compiler_params=pltpu.CompilerParams(vmem_limit_bytes=60 * 1024 * 1024),
     )(codes, notes)
     return value.reshape(rows), image

time: 60.9 us -> 61.7 us (1.013)
    pallas_call x1, Pallas kernels: 2 us -> 3.36 us  [per_device(): pl.pallas_call(functools.partial(decode, share), out_shape=(jax.ShapeDtyp...]
    pallas_call x1, Pallas kernels: 58.2 us -> 57.2 us  [per_device(): pl.pallas_call(functools.partial(kernel, (nsrc, ntgt, eps)), out_shape=(j...]
where the time goes in v6:
time: 61.7 us; the launch traced here: 61.2 us
  Pallas kernels  60.6 us (98%)
  between operations  0.64 us (1%)
    pallas_call x1, Pallas kernels, per_device(): pl.pallas_call(functools.partial(kernel, (nsrc, ntgt, eps)), out_shape=(j...  57.2 us
    pallas_call x1, Pallas kernels, per_device(): pl.pallas_call(functools.partial(decode, share), out_shape=(jax.ShapeDtyp...  3.36 us

profile of v6, /device:TPU:1, one launch (start us, length us, event | category | flops | bytes accessed | tf_op | source)
XLA Modules:
  0.0 61.2 jit_solution(4948633385247943058)
XLA Ops:
  0.6 57.2 %shard_map.59 = (s16[512,256]{1,0:T(8,128)(2,1)}, f32[8,8,128]{2,1,0:T(8,128)}) custom-call(bf16[512,256]{1,0:T(8,128)(2,1)} %src_hbm.1, bf16[512,256]{1,0:T(8,128)(2,1)} %tgt_hbm.1, f32[1,512]{1,0:T(1,128)} %bitcast.2, s32[4,512]{1,0:T(4,128)} %act_hbm.1), custom_call_target="tpu_custom_call" | custom-call | tf_op jit(solution)/shard_map/pallas_call | solution.py:476
  57.8 3.4 %shard_map.60 = (f32[4,128]{1,0:T(4,128)}, f32[512,256]{1,0:T(8,128)}) custom-call(s16[512,256]{1,0:T(8,128)(2,1)} %get-tuple-element.6.code_ref, f32[8,8,128]{2,1,0:T(8,128)} %get-tuple-element.7.note_ref), custom_call_target="tpu_custom_call" | custom-call | tf_op jit(solution)/shard_map/pallas_call | solution.py:521

commit v7 on v6

--- a/solution.py
+++ b/solution.py
@@ -15,7 +15,7 @@
 
 
 def kernel(sizes, src_hbm, tgt_hbm, pot_hbm, act_hbm, code_ref, note_ref,
-           src, pot, act, local, held, scores, weights, crossed, spread, top, rescale, total, turned, pairtop, pairturned, coded, mask, norm, stat,
+           src, flat, pot, act, local, held, scores, weights, crossed, spread, top, rescale, total, turned, pairtop, pairturned, coded, mask, norm, stat,
            gotstat, gotnum, factor, recv, send_z, send_x, pair_recv, pair_send, rs_recv, rs_send, ag_recv, ag_send):
     nsrc, ntgt, eps = sizes
     rows, width = src_hbm.shape
@@ -91,6 +91,7 @@
 
     ones = jnp.ones((8, width), BF16)
     across = (((1,), (1,)), ((), ()))
+    along = (((1,), (0,)), ((), ()))
 
     def half_norms(block_rows):
         wide = block_rows.astype(F32)
@@ -178,7 +179,9 @@
     share_active.wait_recv()
     set_mask(1)
     share_sources.wait_recv()
-    src[...] = (src[...].astype(F32) * (1.0 / eps)).astype(BF16)
+    for b in range(2 * sblocks):
+        at = slice(b * block, (b + 1) * block)
+        flat[:, at] = (src[at, :].astype(F32) * (1.0 / eps)).T.astype(BF16)
 
     tile = scores.shape[2]
     per = block // 8
@@ -188,7 +191,7 @@
 
     def score_piece(k, lane, n, maxima):
         product = lax.dot_general(
-            points(k, lane), src[n * tile:(n + 1) * tile, :], across, preferred_element_type=F32
+            points(k, lane), flat[:, n * tile:(n + 1) * tile], along, preferred_element_type=F32
         )
         for h in range(piece // block):
             shifts = spread[lane * piece + h * block:lane * piece + (h + 1) * block, :]
@@ -210,9 +213,9 @@
         for h in range(piece // block):
             for c in range(tile // block):
                 spot = lane * piece + h * block
-                against = jnp.where(bit(k, lane, h, n * (tile // block) + c), tops[c], -LOWEST)
+                against = jnp.where(bit(k, lane, h, n * (tile // block) + c), tops[c] * to_two, -LOWEST)
                 score = scores[n, spot:spot + block, c * block:(c + 1) * block]
-                weight = jnp.exp2((score - against) * to_two)
+                weight = jnp.exp2(score * to_two - against)
                 sums[c] = sums[c] + jnp.sum(weight.reshape(per, 8, block), axis=0)
                 weights[n, spot:spot + block, c * block:(c + 1) * block] = weight.astype(BF16)
 
@@ -450,16 +453,16 @@
 def decode(share, code_ref, note_ref, val_ref, map_ref):
     block = 128
     lane = lax.broadcasted_iota(jnp.int32, (1, block), 1)
-    b = pl.program_id(0)
-
-    @pl.when(b == 0)
-    def _():
-        for at in range(val_ref.shape[0]):
-            val_ref[at:at + 1, :] = jnp.where(lane < share, note_ref[2 * at, 0:1, :], note_ref[2 * at + 1, 0:1, :])
-
-    bound = jnp.where(lane < share, note_ref[2 * b, 1:2, :], note_ref[2 * b + 1, 1:2, :])
-    column = jnp.broadcast_to(bound, (block, block)).T
-    map_ref[...] = code_ref[...].astype(jnp.int32).astype(F32) * (1.0 / 32767.0) * column[:, 0:1]
+    blocks = range(val_ref.shape[0])
+    bounds = []
+    for b in blocks:
+        first, second = note_ref[2 * b], note_ref[2 * b + 1]
+        val_ref[b:b + 1, :] = jnp.where(lane < share, first[0:1, :], second[0:1, :])
+        bounds.append(jnp.where(lane < share, first[1:2, :], second[1:2, :]))
+    column = jnp.concatenate(bounds + [jnp.zeros((block - len(bounds), block), F32)], axis=0).T
+    for b in blocks:
+        at = slice(b * block, (b + 1) * block)
+        map_ref[at, :] = code_ref[at, :].astype(jnp.int32).astype(F32) * (1.0 / 32767.0) * column[:, b:b + 1]
 
 
 def per_device(sources, targets, target_potential, active):
@@ -483,6 +486,7 @@
         out_specs=(vmem, vmem),
         scratch_shapes=[
             pltpu.VMEM((2 * rows, width), BF16),
+            pltpu.VMEM((width, 2 * rows), BF16),
             pltpu.VMEM((1, count), F32),
             pltpu.VMEM((2,) + active.shape, jnp.int32),
             dma((4, 2)),
@@ -524,15 +528,6 @@
             jax.ShapeDtypeStruct((sblocks, 128), F32),
             jax.ShapeDtypeStruct((rows, width), F32),
         ),
-        grid=(sblocks,),
-        in_specs=[
-            pl.BlockSpec((128, width), lambda b: (b, 0)),
-            pl.BlockSpec((nsrc, 8, 128), lambda b: (0, 0, 0)),
-        ],
-        out_specs=(
-            pl.BlockSpec((sblocks, 128), lambda b: (0, 0)),
-            pl.BlockSpec((128, width), lambda b: (b, 0)),
-        ),
         compiler_params=pltpu.CompilerParams(vmem_limit_bytes=60 * 1024 * 1024),
     )(codes, notes)
     return value.reshape(rows), image

time: 61.7 us -> 60.3 us (0.977)
  Pallas kernels: 60.6 us -> 59.2 us
    pallas_call x1, Pallas kernels: 3.36 us -> 2 us  [per_device(): pl.pallas_call(functools.partial(decode, share), out_shape=(jax.ShapeDtyp...]
where the time goes in v7:
time: 60.3 us; the launch traced here: 59.8 us
  Pallas kernels  59.2 us (98%)
  between operations  0.64 us (1%)
    pallas_call x1, Pallas kernels, per_device(): pl.pallas_call(functools.partial(kernel, (nsrc, ntgt, eps)), out_shape=(j...  57.2 us
    pallas_call x1, Pallas kernels, per_device(): pl.pallas_call(functools.partial(decode, share), out_shape=(jax.ShapeDtyp...  2 us

profile of v7, /device:TPU:1, one launch (start us, length us, event | category | flops | bytes accessed | tf_op | source)
XLA Modules:
  0.0 59.8 jit_solution(6331891642283421866)
XLA Ops:
  0.6 57.2 %shard_map.59 = (s16[512,256]{1,0:T(8,128)(2,1)}, f32[8,8,128]{2,1,0:T(8,128)}) custom-call(bf16[512,256]{1,0:T(8,128)(2,1)} %src_hbm.1, bf16[512,256]{1,0:T(8,128)(2,1)} %tgt_hbm.1, f32[1,512]{1,0:T(1,128)} %bitcast.2, s32[4,512]{1,0:T(4,128)} %act_hbm.1), custom_call_target="tpu_custom_call" | custom-call | tf_op jit(solution)/shard_map/pallas_call | solution.py:479
  57.8 2.0 %shard_map.60 = (f32[4,128]{1,0:T(4,128)}, f32[512,256]{1,0:T(8,128)}) custom-call(s16[512,256]{1,0:T(8,128)(2,1)} %get-tuple-element.6.code_ref, f32[8,8,128]{2,1,0:T(8,128)} %get-tuple-element.7.note_ref), custom_call_target="tpu_custom_call" | custom-call | tf_op jit(solution)/shard_map/pallas_call | solution.py:525

commit v8 on v7

--- a/solution.py
+++ b/solution.py
@@ -15,7 +15,7 @@
 
 
 def kernel(sizes, src_hbm, tgt_hbm, pot_hbm, act_hbm, code_ref, note_ref,
-           src, flat, pot, act, local, held, scores, weights, crossed, spread, top, rescale, total, turned, pairtop, pairturned, coded, mask, norm, stat,
+           src, flat, pot, act, local, held, offsets, scores, weights, crossed, spread, top, rescale, total, turned, pairtop, pairturned, coded, mask, norm, stat,
            gotstat, gotnum, factor, recv, send_z, send_x, pair_recv, pair_send, rs_recv, rs_send, ag_recv, ag_send):
     nsrc, ntgt, eps = sizes
     rows, width = src_hbm.shape
@@ -46,7 +46,7 @@
 
     loads = [
         pltpu.make_async_copy(tgt_hbm.at[part * piece + h * block:part * piece + (h + 1) * block, :],
-                              held.at[0, 1 - part, h * (block + 16):h * (block + 16) + block, :], local.at[part, h])
+                              held.at[0, 1 - part, h * block:(h + 1) * block, :], local.at[part, h])
         for part in range(2) for h in range(2)
     ] + [
         pltpu.make_async_copy(pot_hbm, pot, local.at[2, 0]),
@@ -61,33 +61,43 @@
             src_ref=source, dst_ref=target, send_sem=ssem, recv_sem=rsem, device_id=device, device_id_type=MESH
         )
 
-    parts_of = (slice(0, block + 16), slice(block + 16, 2 * block + 16))
+    def send(k, lane, to, to_lane, ssem, g, device):
+        rsem = recv.at[to, to_lane, g]
+        if g == 2:
+            return remote(offsets.at[k, lane], offsets.at[to, to_lane], ssem, rsem, device)
+        rows_of = slice(g * block, (g + 1) * block)
+        source = held.at[k, lane, rows_of, :]
+        if isinstance(k, int) and k == 0:
+            first = (1 - lane) * piece + g * block
+            source = tgt_hbm.at[first:first + block, :]
+        return remote(source, held.at[to, to_lane, rows_of, :], ssem, rsem, device)
 
     def send_up(k, lane, to, g):
-        return remote(held.at[k, lane, parts_of[g], :], held.at[to, 0, parts_of[g], :],
-                      send_z.at[0, to, g], recv.at[to, 0, g], up)
+        return send(k, lane, to, 0, send_z.at[0, to, g], g, up)
 
     def send_down(k, lane, to, g):
-        return remote(held.at[k, lane, parts_of[g], :], held.at[to, 1, parts_of[g], :],
-                      send_z.at[1, to, g], recv.at[to, 1, g], down)
+        return send(k, lane, to, 1, send_z.at[1, to, g], g, down)
 
     def send_a(k, lane, g):
-        return remote(held.at[k, lane, parts_of[g], :], held.at[k + 1, 2, parts_of[g], :],
-                      send_x.at[0, k, g], recv.at[k + 1, 2, g], side_a)
+        return send(k, lane, k + 1, 2, send_x.at[0, k, g], g, side_a)
 
     def send_b(k, lane, g):
-        return remote(held.at[k, lane, parts_of[g], :], held.at[k + 1, 3, parts_of[g], :],
-                      send_x.at[1, k, g], recv.at[k + 1, 3, g], side_b)
+        return send(k, lane, k + 1, 3, send_x.at[1, k, g], g, side_b)
 
     share_sources = remote(src_hbm, src.at[rows:2 * rows, :], pair_send.at[0, 0], pair_recv.at[0, 0], twin)
     share_active = remote(act_hbm, act.at[1], pair_send.at[1, 0], pair_recv.at[1, 0], twin)
 
     def arrived(k, lane, g):
-        here = held.at[k, lane, parts_of[g], :]
+        here = offsets.at[k, lane] if g == 2 else held.at[k, lane, g * block:(g + 1) * block, :]
         remote(here, here, send_z.at[0, 0, g], recv.at[k, lane, g], up).wait_recv()
 
-    def points(k, lane):
-        return jnp.concatenate([held[k, lane, 0:block, :], held[k, lane, block + 16:2 * block + 16, :]], axis=0)
+    pl.semaphore_wait(barrier, 5 + nsrc - 1)
+    for g in range(2):
+        send_up(0, 1, 1, g).start()
+        send_down(0, 0, 1, g).start()
+        send_a(0, 1, g).start()
+        send_b(0, 0, g).start()
+    share_sources.start()
 
     ones = jnp.ones((8, width), BF16)
     across = (((1,), (1,)), ((), ()))
@@ -102,40 +112,20 @@
             ones, low, across, preferred_element_type=F32
         )
 
-    own_row = lax.broadcasted_iota(jnp.int32, (8, piece), 0) == lax.broadcasted_iota(jnp.int32, (8, piece), 1) % 8
-    chooser = jnp.where(
-        lax.broadcasted_iota(jnp.int32, (piece, block), 0) // 8 == lax.broadcasted_iota(jnp.int32, (piece, block), 1),
-        1.0, 0.0,
-    ).astype(BF16)
-
     for part in range(2):
         loads[2 * part].wait()
         loads[2 * part + 1].wait()
         if part == 0:
             loads[4].wait()
-        data = points(0, 1 - part)
+        data = held[0, 1 - part, :, :]
         shifted = (pot[0:1, part * piece:(part + 1) * piece] - half_norms(data)[0:1, :]) * (1.0 / eps)
-        high = shifted.astype(BF16).astype(F32)
-        middle = (shifted - high).astype(BF16).astype(F32)
-        low = shifted - high - middle
-        spread_out = [
-            jnp.dot(jnp.where(own_row, jnp.broadcast_to(value, (8, piece)), 0.0).astype(BF16), chooser,
-                    preferred_element_type=F32)
-            for value in (high, middle, low)
-        ]
-        extra = jnp.concatenate([
-            jnp.concatenate([spread_out[0], spread_out[1]], axis=1),
-            jnp.concatenate([spread_out[2], jnp.zeros((8, block), F32)], axis=1),
-        ], axis=0)
-        held[0, 1 - part, block:block + 16, :] = extra.astype(BF16)
-
-    pl.semaphore_wait(barrier, 5 + nsrc - 1)
-    for g in range(2):
-        send_up(0, 1, 1, g).start()
-        send_down(0, 0, 1, g).start()
-        send_a(0, 1, g).start()
-        send_b(0, 0, g).start()
-    share_sources.start()
+        for h in range(2):
+            offsets[0, 1 - part, h:h + 1, :] = shifted[:, h * block:(h + 1) * block]
+
+    send_up(0, 1, 1, 2).start()
+    send_down(0, 0, 1, 2).start()
+    send_a(0, 1, 2).start()
+    send_b(0, 0, 2).start()
     share_active.start()
 
     loads[5].wait()
@@ -171,7 +161,7 @@
     rescale[...] = jnp.ones(rescale.shape, F32)
     total[...] = jnp.zeros(total.shape, F32)
     turned[...] = jnp.zeros(turned.shape, F32)
-    for g in range(2):
+    for g in (2, 0, 1):
         send_up(0, 1, 1, g).wait_send()
         send_up(0, 0, 2, g).start()
         send_down(0, 0, 1, g).wait_send()
@@ -191,7 +181,7 @@
 
     def score_piece(k, lane, n, maxima):
         product = lax.dot_general(
-            points(k, lane), flat[:, n * tile:(n + 1) * tile], along, preferred_element_type=F32
+            held[k, lane, :, :], flat[:, n * tile:(n + 1) * tile], along, preferred_element_type=F32
         )
         for h in range(piece // block):
             shifts = spread[lane * piece + h * block:lane * piece + (h + 1) * block, :]
@@ -204,10 +194,9 @@
                 maxima[c] = jnp.maximum(maxima[c], best)
 
     def spread_shifts(k, lane):
-        extra = held[k, lane, block:block + 16, :].astype(F32)
-        shift = extra[0:8, 0:block] + extra[0:8, block:2 * block] + extra[8:16, 0:block]
-        for q in range(piece // 8):
-            spread[lane * piece + 8 * q:lane * piece + 8 * q + 8, :] = jnp.broadcast_to(shift[:, q:q + 1], (8, block))
+        for h in range(piece // block):
+            spot = lane * piece + h * block
+            spread[spot:spot + block, :] = jnp.broadcast_to(offsets[k, lane, h:h + 1, :], (block, block)).T
 
     def weigh_piece(k, lane, n, tops, sums):
         for h in range(piece // block):
@@ -226,7 +215,7 @@
 
     def cross(k, lanes):
         for lane in lanes:
-            crossed[:, lane * piece:(lane + 1) * piece] = points(k, lane).T
+            crossed[:, lane * piece:(lane + 1) * piece] = held[k, lane, :, :].T
 
     def absorb(fresh, ready, tick=None, fresh_lanes=everything, ready_lanes=everything):
         if ready is not None:
@@ -304,14 +293,14 @@
 
     def sides(k):
         for lane in (2, 3):
-            for g in range(2):
+            for g in (2, 0, 1):
                 arrived(k, lane, g)
 
     def tick_of(k):
         def tick(n):
-            if n % 2 == 0:
+            for g in ((2, 0), (), (1,), ())[n]:
                 for lane in range(2):
-                    pass_on(k, lane, n // 2)
+                    pass_on(k, lane, g)
         return tick
 
     absorb(0, None, tick_of(jnp.int32(1)), fresh_lanes=(0, 1))
@@ -419,14 +408,14 @@
     for d in range(1, nsrc):
         spread_rows(d).start()
 
-    for g in range(2):
+    for g in range(3):
         send_up(0, 0, 2, g).wait_send()
         send_down(0, 1, 2, g).wait_send()
         send_a(0, 1, g).wait_send()
         send_b(0, 0, g).wait_send()
 
     def drain(k, carry):
-        for g in range(2):
+        for g in range(3):
             @pl.when(k + 2 < rounds)
             def _():
                 send_up(k, 0, k + 2, g).wait_send()
@@ -490,7 +479,8 @@
             pltpu.VMEM((1, count), F32),
             pltpu.VMEM((2,) + active.shape, jnp.int32),
             dma((4, 2)),
-            pltpu.VMEM((rounds + 1, 4, piece + 16, width), BF16),
+            pltpu.VMEM((rounds + 1, 4, piece, width), BF16),
+            pltpu.VMEM((rounds + 1, 4, 2, 128), F32),
             pltpu.VMEM((2 * rows // 256, 4 * piece, 256), F32),
             pltpu.VMEM((2 * rows // 256, 4 * piece, 256), BF16),
             pltpu.VMEM((width, 4 * piece), BF16),
@@ -508,9 +498,9 @@
             pltpu.VMEM((nsrc, 8, 128), F32),
             pltpu.VMEM((nsrc, share, width), jnp.int16),
             pltpu.VMEM((128, 128), F32),
-            dma((rounds + 1, 4, 2)),
-            dma((2, rounds, 2)),
-            dma((2, rounds, 2)),
+            dma((rounds + 1, 4, 3)),
+            dma((2, rounds, 3)),
+            dma((2, rounds, 3)),
             dma((4, 2)),
             dma((4, 2)),
             dma((2, nsrc)),

time: 60.3 us -> 60.3 us (level)
  no operation moved by 1% of the time
where the time goes in v8:
time: 60.3 us; the launch traced here: 59.8 us
  Pallas kernels  59.1 us (98%)
  between operations  0.64 us (1%)
    pallas_call x1, Pallas kernels, per_device(): pl.pallas_call(functools.partial(kernel, (nsrc, ntgt, eps)), out_shape=(j...  57.1 us
    pallas_call x1, Pallas kernels, per_device(): pl.pallas_call(functools.partial(decode, share), out_shape=(jax.ShapeDtyp...  2 us

profile of v8, /device:TPU:1, one launch (start us, length us, event | category | flops | bytes accessed | tf_op | source)
XLA Modules:
  0.0 59.8 jit_solution(16690084928674833066)
XLA Ops:
  0.6 57.1 %shard_map.59 = (s16[512,256]{1,0:T(8,128)(2,1)}, f32[8,8,128]{2,1,0:T(8,128)}) custom-call(bf16[512,256]{1,0:T(8,128)(2,1)} %src_hbm.1, bf16[512,256]{1,0:T(8,128)(2,1)} %tgt_hbm.1, f32[1,512]{1,0:T(1,128)} %bitcast.2, s32[4,512]{1,0:T(4,128)} %act_hbm.1), custom_call_target="tpu_custom_call" | custom-call | tf_op jit(solution)/shard_map/pallas_call | solution.py:468
  57.8 2.0 %shard_map.60 = (f32[4,128]{1,0:T(4,128)}, f32[512,256]{1,0:T(8,128)}) custom-call(s16[512,256]{1,0:T(8,128)(2,1)} %get-tuple-element.6.code_ref, f32[8,8,128]{2,1,0:T(8,128)} %get-tuple-element.7.note_ref), custom_call_target="tpu_custom_call" | custom-call | tf_op jit(solution)/shard_map/pallas_call | solution.py:515

commit v9 on v8

--- a/solution.py
+++ b/solution.py
@@ -139,7 +139,7 @@
     part_h, kind, k = place % 2, (place // 2) % 4, place // 8
     from_side = kind >= 2
     k = jnp.where(from_side, k - 1, k)
-    odd = k % 2
+    odd = (k + 2) % 2
     distance = (k + 1) // 2
     below = jnp.where(kind == 0, 1, jnp.where(kind == 1, 0, jnp.where(kind == 2, odd, 1 - odd)))
     letter = jnp.where(kind == 0, 1 - odd, jnp.where(kind == 1, odd, kind - 2))
@@ -147,7 +147,7 @@
     x_lo_from = jnp.where(from_side, 1 - x_lo, x_lo)
     x_hi_from = jnp.where(kind == 3, 1 - x_hi, x_hi)
     owner = (x_hi_from * half + y) * ntgt + z_from * 4 + x_lo_from * 2 + core
-    number = owner * 4 + letter * 2 + part_h
+    number = jnp.where(k < 0, -1, owner * 4 + letter * 2 + part_h)
 
     def set_mask(part):
         for b in range(sblocks):
@@ -157,6 +157,8 @@
             mask[part * sblocks + b] = jnp.broadcast_to(jnp.max(hit, axis=1, keepdims=True), (slots, block))
 
     set_mask(0)
+    held[0, 2:4, :, :] = jnp.zeros((2, piece, width), BF16)
+    offsets[0, 2:4, :, :] = jnp.zeros((2, 2, block), F32)
     top[...] = jnp.full(top.shape, LOWEST, F32)
     rescale[...] = jnp.ones(rescale.shape, F32)
     total[...] = jnp.zeros(total.shape, F32)
@@ -169,19 +171,26 @@
     share_active.wait_recv()
     set_mask(1)
     share_sources.wait_recv()
-    for b in range(2 * sblocks):
-        at = slice(b * block, (b + 1) * block)
-        flat[:, at] = (src[at, :].astype(F32) * (1.0 / eps)).T.astype(BF16)
-
     tile = scores.shape[2]
+    tiles = 2 * rows // tile
+
+    def flatten(n, carry):
+        data = src[pl.ds(pl.multiple_of(n * tile, tile), tile), :]
+        flat[n] = (data.astype(F32) * (1.0 / eps)).T.astype(BF16)
+        return carry
+
+    lax.fori_loop(0, tiles, flatten, 0)
+
     per = block // 8
+    inside = range(tile // block)
+    cut = [slice(c * block, (c + 1) * block) for c in inside]
 
     def bit(k, lane, h, b):
         return mask[b, pl.ds((k * 4 + lane) * 2 + h, 1), :] > 0.5
 
     def score_piece(k, lane, n, maxima):
         product = lax.dot_general(
-            held[k, lane, :, :], flat[:, n * tile:(n + 1) * tile], along, preferred_element_type=F32
+            held[k, lane, :, :], flat[n], along, preferred_element_type=F32
         )
         for h in range(piece // block):
             shifts = spread[lane * piece + h * block:lane * piece + (h + 1) * block, :]
@@ -208,72 +217,72 @@
                 sums[c] = sums[c] + jnp.sum(weight.reshape(per, 8, block), axis=0)
                 weights[n, spot:spot + block, c * block:(c + 1) * block] = weight.astype(BF16)
 
-    def columns(n, c):
-        return slice(n * tile + c * block, n * tile + (c + 1) * block)
-
-    everything = (0, 1, 2, 3)
-
     def cross(k, lanes):
         for lane in lanes:
             crossed[:, lane * piece:(lane + 1) * piece] = held[k, lane, :, :].T
 
-    def absorb(fresh, ready, tick=None, fresh_lanes=everything, ready_lanes=everything):
+    def absorb(fresh, ready, tick=None):
         if ready is not None:
-            cross(ready, ready_lanes)
+            cross(ready, range(4))
         if fresh is not None:
-            for lane in fresh_lanes:
+            for lane in range(4):
                 spread_shifts(fresh, lane)
-        parts = range(tile // block)
-        for n in range(2 * rows // tile):
+
+        def one_tile(n, carry):
             if tick is not None:
                 tick(n)
-            tops = [top[0:1, columns(n, c)] for c in parts]
+            tops = [top[n, 0:1, cut[c]] for c in inside]
             maxima = list(tops)
-            scales = [rescale[0:1, columns(n, c)] for c in parts]
-            sums = [total[:, columns(n, c)] * scales[c] for c in parts]
+            scales = [rescale[n, 0:1, cut[c]] for c in inside]
+            sums = [total[n, :, cut[c]] * scales[c] for c in inside]
             added = None
             for lane in range(4):
-                if ready is not None and lane in ready_lanes:
+                if ready is not None:
                     weigh_piece(ready, lane, n, tops, sums)
-                if fresh is not None and lane in fresh_lanes:
+                if fresh is not None:
                     score_piece(fresh, lane, n, maxima)
-                if ready is not None and lane in ready_lanes and lane % 2 == 1:
+                if ready is not None and lane % 2 == 1:
                     span = slice((lane - 1) * piece, (lane + 1) * piece)
                     term = jnp.dot(crossed[:, span], weights[n, span, :], preferred_element_type=F32)
                     added = term if added is None else added + term
-            for c in parts:
-                at = columns(n, c)
+            for c in inside:
                 if ready is not None:
-                    total[:, at] = sums[c]
-                    turned[:, at] = turned[:, at] * scales[c] + added[:, c * block:(c + 1) * block]
+                    total[n, :, cut[c]] = sums[c]
+                    turned[n, :, cut[c]] = turned[n, :, cut[c]] * scales[c] + added[:, cut[c]]
                 if fresh is not None:
                     new = jnp.max(maxima[c], axis=0, keepdims=True)
-                    rescale[0:1, at] = jnp.exp2((tops[c] - new) * to_two)
-                    top[0:1, at] = new
+                    rescale[n, 0:1, cut[c]] = jnp.exp2((tops[c] - new) * to_two)
+                    top[n, 0:1, cut[c]] = new
+            return carry
+
+        lax.fori_loop(0, tiles, one_tile, 0)
 
     def finish(k, after):
         cross(k, (2, 3))
         for lane in (2, 3):
             spread_shifts(k, lane)
-        parts = range(tile // block)
         span = slice(2 * piece, 4 * piece)
-        for n in (2, 3, 0, 1):
-            tops = [top[0:1, columns(n, c)] for c in parts]
+
+        def one_tile(i, carry):
+            n = (i + tiles // 2) % tiles
+            tops = [top[n, 0:1, cut[c]] for c in inside]
             maxima = list(tops)
             for lane in (2, 3):
                 score_piece(k, lane, n, maxima)
-            new = [jnp.max(maxima[c], axis=0, keepdims=True) for c in parts]
-            scales = [jnp.exp2((tops[c] - new[c]) * to_two) for c in parts]
-            sums = [total[:, columns(n, c)] * scales[c] for c in parts]
+            new = [jnp.max(maxima[c], axis=0, keepdims=True) for c in inside]
+            scales = [jnp.exp2((tops[c] - new[c]) * to_two) for c in inside]
+            sums = [total[n, :, cut[c]] * scales[c] for c in inside]
             for lane in (2, 3):
                 weigh_piece(k, lane, n, new, sums)
             added = jnp.dot(crossed[:, span], weights[n, span, :], preferred_element_type=F32)
-            for c in parts:
-                at = columns(n, c)
-                top[0:1, at] = new[c]
-                top[1:2, at] = jnp.sum(sums[c], axis=0, keepdims=True)
-                turned[:, at] = turned[:, at] * scales[c] + added[:, c * block:(c + 1) * block]
+            for c in inside:
+                top[n, 0:1, cut[c]] = new[c]
+                top[n, 1:2, cut[c]] = jnp.sum(sums[c], axis=0, keepdims=True)
+                turned[n, :, cut[c]] = turned[n, :, cut[c]] * scales[c] + added[:, cut[c]]
             after(n)
+            return carry
+
+        lax.fori_loop(0, tiles, one_tile, 0)
 
     def pass_on(k, lane, g):
         onward = (send_up, send_down)[lane]
@@ -298,31 +307,29 @@
 
     def tick_of(k):
         def tick(n):
-            for g in ((2, 0), (), (1,), ())[n]:
-                for lane in range(2):
-                    pass_on(k, lane, g)
+            for when, gs in ((0, (2, 0)), (tiles // 2, (1,))):
+                @pl.when(jnp.logical_and(n == when, k < rounds))
+                def _():
+                    for g in gs:
+                        for lane in range(2):
+                            pass_on(k, lane, g)
         return tick
 
-    absorb(0, None, tick_of(jnp.int32(1)), fresh_lanes=(0, 1))
-    sides(1)
-    absorb(1, 0, tick_of(jnp.int32(2)), ready_lanes=(0, 1))
+    absorb(0, None, tick_of(jnp.int32(1)))
 
     def one_round(k, carry):
         sides(k - 1)
         absorb(k - 1, k - 2, tick_of(k))
         return carry
 
-    lax.fori_loop(3, rounds, one_round, 0)
-    sides(rounds - 1)
-    absorb(rounds - 1, rounds - 2)
+    lax.fori_loop(2, rounds + 1, one_round, 0)
     absorb(None, rounds - 1)
     sides(rounds)
 
     def pair_copies(i):
-        at = slice(rows + i * tile, rows + (i + 1) * tile)
         return (
-            remote(top.at[:, at], pairtop.at[i], pair_send.at[2, i], pair_recv.at[2, i], twin),
-            remote(turned.at[:, at], pairturned.at[i], pair_send.at[3, i], pair_recv.at[3, i], twin),
+            remote(top.at[i + tiles // 2], pairtop.at[i], pair_send.at[2, i], pair_recv.at[2, i], twin),
+            remote(turned.at[i + tiles // 2], pairturned.at[i], pair_send.at[3, i], pair_recv.at[3, i], twin),
         )
 
     def share_of(q):
@@ -334,18 +341,19 @@
     def give_rows(q, d):
         return remote(coded.at[share_of(q), :], gotnum.at[d], rs_send.at[1, d], rs_recv.at[1, d], (q, t))
 
-    def merge(b):
-        i, inside = b // (tile // block), slice(b % (tile // block) * block, (b % (tile // block) + 1) * block)
-        at = slice(b * block, (b + 1) * block)
-        best = jnp.maximum(top[0:1, at], pairtop[i, 0:1, inside])
-        ours = jnp.exp2((top[0:1, at] - best) * to_two)
-        theirs = jnp.exp2((pairtop[i, 0:1, inside] - best) * to_two)
-        both = turned[:, at] * ours + pairturned[i, :, inside] * theirs
+    def merge(n, c):
+        b = n * (tile // block) + c
+        best = jnp.maximum(top[n, 0:1, cut[c]], pairtop[n, 0:1, cut[c]])
+        ours = jnp.exp2((top[n, 0:1, cut[c]] - best) * to_two)
+        theirs = jnp.exp2((pairtop[n, 0:1, cut[c]] - best) * to_two)
+        both = turned[n, :, cut[c]] * ours + pairturned[n, :, cut[c]] * theirs
         largest = jnp.maximum(jnp.max(jnp.abs(both), axis=0, keepdims=True), 2e-38)
         stat[b, 0:1, :] = best
-        stat[b, 1:2, :] = top[1:2, at] * ours + pairtop[i, 1:2, inside] * theirs
+        stat[b, 1:2, :] = top[n, 1:2, cut[c]] * ours + pairtop[n, 1:2, cut[c]] * theirs
         stat[b, 2:3, :] = largest
-        coded[at, :] = jnp.round((both * (1.0 / largest) * 32767.0).T).astype(jnp.int32).astype(jnp.int16)
+        coded[pl.ds(pl.multiple_of(b * block, block), block), :] = jnp.round(
+            (both * (1.0 / largest) * 32767.0).T
+        ).astype(jnp.int32).astype(jnp.int16)
         for q in (2 * b, 2 * b + 1):
             d = (q - s + nsrc) % nsrc
 
@@ -355,15 +363,19 @@
                 give_rows(q, d).start()
 
     def after(n):
-        own = rows // tile
-        if n >= own:
+        own = tiles // 2
+
+        @pl.when(n >= own)
+        def _():
             for copy in pair_copies(n - own):
                 copy.start()
-        else:
+
+        @pl.when(n < own)
+        def _():
             for copy in pair_copies(n):
                 copy.wait_recv()
-            for c in range(tile // block):
-                merge(n * (tile // block) + c)
+            for c in inside:
+                merge(n, c)
 
     finish(rounds, after)
 
@@ -475,7 +487,7 @@
         out_specs=(vmem, vmem),
         scratch_shapes=[
             pltpu.VMEM((2 * rows, width), BF16),
-            pltpu.VMEM((width, 2 * rows), BF16),
+            pltpu.VMEM((2 * rows // 256, width, 256), BF16),
             pltpu.VMEM((1, count), F32),
             pltpu.VMEM((2,) + active.shape, jnp.int32),
             dma((4, 2)),
@@ -485,10 +497,10 @@
             pltpu.VMEM((2 * rows // 256, 4 * piece, 256), BF16),
             pltpu.VMEM((width, 4 * piece), BF16),
             pltpu.VMEM((4 * piece, 128), F32),
-            pltpu.VMEM((8, 2 * rows), F32),
-            pltpu.VMEM((8, 2 * rows), F32),
-            pltpu.VMEM((8, 2 * rows), F32),
-            pltpu.VMEM((width, 2 * rows), F32),
+            pltpu.VMEM((2 * rows // 256, 8, 256), F32),
+            pltpu.VMEM((2 * rows // 256, 8, 256), F32),
+            pltpu.VMEM((2 * rows // 256, 8, 256), F32),
+            pltpu.VMEM((2 * rows // 256, width, 256), F32),
             pltpu.VMEM((rows // 256, 8, 256), F32),
             pltpu.VMEM((rows // 256, width, 256), F32),
             pltpu.VMEM((rows, width), jnp.int16),

time: 60.3 us -> 62.4 us (1.035)
  Pallas kernels: 59.1 us -> 61.4 us
    pallas_call x1, Pallas kernels: 57.1 us -> 59.4 us  [per_device(): pl.pallas_call(functools.partial(kernel, (nsrc, ntgt, eps)), out_shape=(j...]
where the time goes in v9:
time: 62.4 us; the launch traced here: 62.1 us
  Pallas kernels  61.4 us (98%)
  between operations  0.64 us (1%)
    pallas_call x1, Pallas kernels, per_device(): pl.pallas_call(functools.partial(kernel, (nsrc, ntgt, eps)), out_shape=(j...  59.4 us
    pallas_call x1, Pallas kernels, per_device(): pl.pallas_call(functools.partial(decode, share), out_shape=(jax.ShapeDtyp...  2 us

profile of v9, /device:TPU:1, one launch (start us, length us, event | category | flops | bytes accessed | tf_op | source)
XLA Modules:
  0.0 62.1 jit_solution(2537807346318333326)
XLA Ops:
  0.6 59.4 %shard_map.59 = (s16[512,256]{1,0:T(8,128)(2,1)}, f32[8,8,128]{2,1,0:T(8,128)}) custom-call(bf16[512,256]{1,0:T(8,128)(2,1)} %src_hbm.1, bf16[512,256]{1,0:T(8,128)(2,1)} %tgt_hbm.1, f32[1,512]{1,0:T(1,128)} %bitcast.2, s32[4,512]{1,0:T(4,128)} %act_hbm.1), custom_call_target="tpu_custom_call" | custom-call | tf_op jit(solution)/shard_map/pallas_call | solution.py:480
  60.1 2.0 %shard_map.60 = (f32[4,128]{1,0:T(4,128)}, f32[512,256]{1,0:T(8,128)}) custom-call(s16[512,256]{1,0:T(8,128)(2,1)} %get-tuple-element.6.code_ref, f32[8,8,128]{2,1,0:T(8,128)} %get-tuple-element.7.note_ref), custom_call_target="tpu_custom_call" | custom-call | tf_op jit(solution)/shard_map/pallas_call | solution.py:527

commit v10 on v8

--- a/solution.py
+++ b/solution.py
@@ -179,19 +179,22 @@
     def bit(k, lane, h, b):
         return mask[b, pl.ds((k * 4 + lane) * 2 + h, 1), :] > 0.5
 
-    def score_piece(k, lane, n, maxima):
+    def score_pair(k, lane, n, maxima):
+        data = held[k, lane:lane + 2, :, :].reshape(2 * piece, width)
         product = lax.dot_general(
-            held[k, lane, :, :], flat[:, n * tile:(n + 1) * tile], along, preferred_element_type=F32
+            data, flat[:, n * tile:(n + 1) * tile], along, preferred_element_type=F32
         )
-        for h in range(piece // block):
-            shifts = spread[lane * piece + h * block:lane * piece + (h + 1) * block, :]
-            for c in range(tile // block):
-                score = product[h * block:(h + 1) * block, c * block:(c + 1) * block] + shifts
-                spot = lane * piece + h * block
-                scores[n, spot:spot + block, c * block:(c + 1) * block] = score
-                best = jnp.max(score.reshape(per, 8, block), axis=0)
-                best = jnp.where(bit(k, lane, h, n * (tile // block) + c), best, LOWEST)
-                maxima[c] = jnp.maximum(maxima[c], best)
+        for near in (lane, lane + 1):
+            for h in range(piece // block):
+                spot = near * piece + h * block
+                shifts = spread[spot:spot + block, :]
+                for c in range(tile // block):
+                    down = spot - lane * piece
+                    score = product[down:down + block, c * block:(c + 1) * block] + shifts
+                    scores[n, spot:spot + block, c * block:(c + 1) * block] = score
+                    best = jnp.max(score.reshape(per, 8, block), axis=0)
+                    best = jnp.where(bit(k, near, h, n * (tile // block) + c), best, LOWEST)
+                    maxima[c] = jnp.maximum(maxima[c], best)
 
     def spread_shifts(k, lane):
         for h in range(piece // block):
@@ -232,13 +235,14 @@
             scales = [rescale[0:1, columns(n, c)] for c in parts]
             sums = [total[:, columns(n, c)] * scales[c] for c in parts]
             added = None
-            for lane in range(4):
+            for lane in (0, 2):
                 if ready is not None and lane in ready_lanes:
                     weigh_piece(ready, lane, n, tops, sums)
+                    weigh_piece(ready, lane + 1, n, tops, sums)
                 if fresh is not None and lane in fresh_lanes:
-                    score_piece(fresh, lane, n, maxima)
-                if ready is not None and lane in ready_lanes and lane % 2 == 1:
-                    span = slice((lane - 1) * piece, (lane + 1) * piece)
+                    score_pair(fresh, lane, n, maxima)
+                if ready is not None and lane in ready_lanes:
+                    span = slice(lane * piece, (lane + 2) * piece)
                     term = jnp.dot(crossed[:, span], weights[n, span, :], preferred_element_type=F32)
                     added = term if added is None else added + term
             for c in parts:
@@ -260,8 +264,7 @@
         for n in (2, 3, 0, 1):
             tops = [top[0:1, columns(n, c)] for c in parts]
             maxima = list(tops)
-            for lane in (2, 3):
-                score_piece(k, lane, n, maxima)
+            score_pair(k, 2, n, maxima)
             new = [jnp.max(maxima[c], axis=0, keepdims=True) for c in parts]
             scales = [jnp.exp2((tops[c] - new[c]) * to_two) for c in parts]
             sums = [total[:, columns(n, c)] * scales[c] for c in parts]

time: 60.3 us -> 60.4 us (level)
  no operation moved by 1% of the time
where the time goes in v10:
time: 60.4 us; the launch traced here: 60 us
  Pallas kernels  59.3 us (98%)
  between operations  0.64 us (1%)
    pallas_call x1, Pallas kernels, per_device(): pl.pallas_call(functools.partial(kernel, (nsrc, ntgt, eps)), out_shape=(j...  57.3 us
    pallas_call x1, Pallas kernels, per_device(): pl.pallas_call(functools.partial(decode, share), out_shape=(jax.ShapeDtyp...  2 us

profile of v10, /device:TPU:1, one launch (start us, length us, event | category | flops | bytes accessed | tf_op | source)
XLA Modules:
  0.0 60.0 jit_solution(9755825308875189958)
XLA Ops:
  0.6 57.3 %shard_map.59 = (s16[512,256]{1,0:T(8,128)(2,1)}, f32[8,8,128]{2,1,0:T(8,128)}) custom-call(bf16[512,256]{1,0:T(8,128)(2,1)} %src_hbm.1, bf16[512,256]{1,0:T(8,128)(2,1)} %tgt_hbm.1, f32[1,512]{1,0:T(1,128)} %bitcast.2, s32[4,512]{1,0:T(4,128)} %act_hbm.1), custom_call_target="tpu_custom_call" | custom-call | tf_op jit(solution)/shard_map/pallas_call | solution.py:471
  58.0 2.0 %shard_map.60 = (f32[4,128]{1,0:T(4,128)}, f32[512,256]{1,0:T(8,128)}) custom-call(s16[512,256]{1,0:T(8,128)(2,1)} %get-tuple-element.6.code_ref, f32[8,8,128]{2,1,0:T(8,128)} %get-tuple-element.7.note_ref), custom_call_target="tpu_custom_call" | custom-call | tf_op jit(solution)/shard_map/pallas_call | solution.py:518

commit v11 on v8

--- a/solution.py
+++ b/solution.py
@@ -98,6 +98,9 @@
         send_a(0, 1, g).start()
         send_b(0, 0, g).start()
     share_sources.start()
+    for g in range(2):
+        send_up(0, 0, 2, g).start()
+        send_down(0, 1, 2, g).start()
 
     ones = jnp.ones((8, width), BF16)
     across = (((1,), (1,)), ((), ()))
@@ -126,6 +129,8 @@
     send_down(0, 0, 1, 2).start()
     send_a(0, 1, 2).start()
     send_b(0, 0, 2).start()
+    send_up(0, 0, 2, 2).start()
+    send_down(0, 1, 2, 2).start()
     share_active.start()
 
     loads[5].wait()
@@ -161,11 +166,6 @@
     rescale[...] = jnp.ones(rescale.shape, F32)
     total[...] = jnp.zeros(total.shape, F32)
     turned[...] = jnp.zeros(turned.shape, F32)
-    for g in (2, 0, 1):
-        send_up(0, 1, 1, g).wait_send()
-        send_up(0, 0, 2, g).start()
-        send_down(0, 0, 1, g).wait_send()
-        send_down(0, 1, 2, g).start()
     share_active.wait_recv()
     set_mask(1)
     share_sources.wait_recv()
@@ -303,7 +303,10 @@
                     pass_on(k, lane, g)
         return tick
 
-    absorb(0, None, tick_of(jnp.int32(1)), fresh_lanes=(0, 1))
+    absorb(0, None, fresh_lanes=(0, 1))
+    for g in (2, 0, 1):
+        for lane in range(2):
+            pass_on(jnp.int32(1), lane, g)
     sides(1)
     absorb(1, 0, tick_of(jnp.int32(2)), ready_lanes=(0, 1))
 
@@ -409,6 +412,8 @@
         spread_rows(d).start()
 
     for g in range(3):
+        send_up(0, 1, 1, g).wait_send()
+        send_down(0, 0, 1, g).wait_send()
         send_up(0, 0, 2, g).wait_send()
         send_down(0, 1, 2, g).wait_send()
         send_a(0, 1, g).wait_send()

time: 60.3 us -> 63 us (1.045)
  Pallas kernels: 59.1 us -> 61.8 us
    pallas_call x1, Pallas kernels: 57.1 us -> 59.8 us  [per_device(): pl.pallas_call(functools.partial(kernel, (nsrc, ntgt, eps)), out_shape=(j...]
where the time goes in v11:
time: 63 us; the launch traced here: 62.5 us
  Pallas kernels  61.8 us (98%)
  between operations  0.64 us (1%)
    pallas_call x1, Pallas kernels, per_device(): pl.pallas_call(functools.partial(kernel, (nsrc, ntgt, eps)), out_shape=(j...  59.8 us
    pallas_call x1, Pallas kernels, per_device(): pl.pallas_call(functools.partial(decode, share), out_shape=(jax.ShapeDtyp...  2 us

profile of v11, /device:TPU:1, one launch (start us, length us, event | category | flops | bytes accessed | tf_op | source)
XLA Modules:
  0.0 62.5 jit_solution(56605347603999101)
XLA Ops:
  0.6 59.8 %shard_map.59 = (s16[512,256]{1,0:T(8,128)(2,1)}, f32[8,8,128]{2,1,0:T(8,128)}) custom-call(bf16[512,256]{1,0:T(8,128)(2,1)} %src_hbm.1, bf16[512,256]{1,0:T(8,128)(2,1)} %tgt_hbm.1, f32[1,512]{1,0:T(1,128)} %bitcast.2, s32[4,512]{1,0:T(4,128)} %act_hbm.1), custom_call_target="tpu_custom_call" | custom-call | tf_op jit(solution)/shard_map/pallas_call | solution.py:473
  60.5 2.0 %shard_map.60 = (f32[4,128]{1,0:T(4,128)}, f32[512,256]{1,0:T(8,128)}) custom-call(s16[512,256]{1,0:T(8,128)(2,1)} %get-tuple-element.6.code_ref, f32[8,8,128]{2,1,0:T(8,128)} %get-tuple-element.7.note_ref), custom_call_target="tpu_custom_call" | custom-call | tf_op jit(solution)/shard_map/pallas_call | solution.py:520

commit v12 on v8

--- a/solution.py
+++ b/solution.py
@@ -298,7 +298,7 @@
 
     def tick_of(k):
         def tick(n):
-            for g in ((2, 0), (), (1,), ())[n]:
+            for g in ((2, 0), (1,), (), ())[n]:
                 for lane in range(2):
                     pass_on(k, lane, g)
         return tick

time: 60.3 us -> 60.1 us (level)
  no operation moved by 1% of the time
where the time goes in v12:
time: 60.1 us; the launch traced here: 59.6 us
  Pallas kernels  59 us (98%)
  between operations  0.64 us (1%)
    pallas_call x1, Pallas kernels, per_device(): pl.pallas_call(functools.partial(kernel, (nsrc, ntgt, eps)), out_shape=(j...  57 us
    pallas_call x1, Pallas kernels, per_device(): pl.pallas_call(functools.partial(decode, share), out_shape=(jax.ShapeDtyp...  2 us

profile of v12, /device:TPU:1, one launch (start us, length us, event | category | flops | bytes accessed | tf_op | source)
XLA Modules:
  0.0 59.6 jit_solution(2058921272516268243)
XLA Ops:
  0.6 57.0 %shard_map.59 = (s16[512,256]{1,0:T(8,128)(2,1)}, f32[8,8,128]{2,1,0:T(8,128)}) custom-call(bf16[512,256]{1,0:T(8,128)(2,1)} %src_hbm.1, bf16[512,256]{1,0:T(8,128)(2,1)} %tgt_hbm.1, f32[1,512]{1,0:T(1,128)} %bitcast.2, s32[4,512]{1,0:T(4,128)} %act_hbm.1), custom_call_target="tpu_custom_call" | custom-call | tf_op jit(solution)/shard_map/pallas_call | solution.py:468
  57.6 2.0 %shard_map.60 = (f32[4,128]{1,0:T(4,128)}, f32[512,256]{1,0:T(8,128)}) custom-call(s16[512,256]{1,0:T(8,128)(2,1)} %get-tuple-element.6.code_ref, f32[8,8,128]{2,1,0:T(8,128)} %get-tuple-element.7.note_ref), custom_call_target="tpu_custom_call" | custom-call | tf_op jit(solution)/shard_map/pallas_call | solution.py:515
